TPU v7x, 256 devices: a whole 4x4x8 slice. The times are simulated.
256 devices in a mesh: elem: 128 (over y, x, z), lev: 2 (over core).
Axes of the slice: x: 4, y: 4, z: 8, core: 2. Of those that a mesh axis runs over, the one named last changes fastest.
Arguments:
- tracers: bfloat16 [40, 72, 1024, 128], P(None, 'lev', 'elem'), may hold values from -6 to 6
- wind_x: bfloat16 [72, 1024, 128], P('lev', 'elem'), may hold values from -4 to 4
- wind_y: bfloat16 [72, 1024, 128], P('lev', 'elem'), may hold values from -4 to 4
- span_of: int32 [131072, 1], P('elem'), may hold values from 0 to 1023; in each aligned block of 1024 rows (0 to 1023, 1024 to 2047, ...) at most 2 rows name the same one
- inverses: bfloat16 [1024, 72, 72], P('elem'), may hold values from -2 to 2
Outputs:
- diffused: bfloat16 [40, 72, 1024, 128], P(None, 'lev', 'elem')
Inputs may be any that keep to these rules, and one draw needn't show every extreme that they name: `span_of`: among the columns of one index of elem, at most 2 name the same span, a bound that some block reaches of them.
All inputs are finite; a program needn't handle non-finite values.
Results may differ from a plain program's by a relative error of at most 0.0049.
Values may be sent and summed in bfloat16 or wider, within the bound.
No kernel may reach another device: no remote copies, remote signals or barrier semaphores. Data moves between devices by JAX's collectives and lax.ppermute only.
A program may use at most 128 MiB of HBM per device.

v0:
```python
import jax
import jax.numpy as jnp
import numpy as np
from jax import lax
from jax.sharding import PartitionSpec as P

NP = 4
NSUB = 2


time_step = 0.08


def with_halo(value, sides, width):
    for axis, dim in sides:
        size, length = (lax.axis_size(axis), value.shape[dim])
        up = [(i, (i + 1) % size) for i in range(size)]
        down = [(j, i) for i, j in up]
        last = lax.slice_in_dim(value, length - width, length, axis=dim)
        leading = lax.slice_in_dim(value, 0, width, axis=dim)
        before = lax.ppermute(last, axis, up)
        after = lax.ppermute(leading, axis, down)
        value = jnp.concatenate([before, value, after], axis=dim)
    return value


def derivative_table():
    gll_nodes = np.array([-1.0, -1.0 / np.sqrt(5.0), 1.0 / np.sqrt(5.0), 1.0])
    n = gll_nodes.shape[0]
    derivative = np.zeros((n, n))
    for i in range(n):
        for k in range(n):
            if i == k:
                derivative[i, k] = sum(
                    (1.0 / (gll_nodes[i] - gll_nodes[m]) for m in range(n) if m != i)
                )
            else:
                numerator = np.prod(
                    [gll_nodes[i] - gll_nodes[m] for m in range(n) if m != k and m != i]
                )
                denominator = np.prod([gll_nodes[k] - gll_nodes[m] for m in range(n) if m != k])
                derivative[i, k] = numerator / denominator
    return derivative.astype(np.float32)


def advance(field_state, table_x, table_y, winds_x, winds_y):
    groups, levels, width_x, width_y = field_state.shape
    grad_x = jnp.einsum("ik,qlkn->qlin", table_x, field_state, precision=lax.Precision.HIGHEST)
    grad_y = jnp.einsum("qlxk,jk->qlxj", field_state, table_y, precision=lax.Precision.HIGHEST)
    advected = field_state - time_step * (winds_x * grad_x + winds_y * grad_y)
    padded = with_halo(advected, (("elem", 2),), 1)
    following = padded[:, :, 2:]
    preceding = padded[:, :, :-2]
    node_x = (jnp.arange(width_x, dtype=jnp.int32) % NP)[:, None]
    mixed_x = jnp.where(
        node_x == NP - 1,
        0.5 * (advected + following),
        jnp.where(node_x == 0, 0.5 * (preceding + advected), advected),
    )
    following = jnp.roll(mixed_x, -1, axis=3)
    preceding = jnp.roll(mixed_x, 1, axis=3)
    node_y = jnp.arange(width_y, dtype=jnp.int32) % NP
    return jnp.where(
        node_y == NP - 1,
        0.5 * (mixed_x + following),
        jnp.where(node_y == 0, 0.5 * (preceding + mixed_x), mixed_x),
    )


def tracer_split(columns):
    return lax.all_to_all(columns, "lev", split_axis=0, concat_axis=1, tiled=True)


def level_return(columns):
    return lax.all_to_all(columns, "lev", split_axis=1, concat_axis=0, tiled=True)


def slot_index(span_ids, capacity, per_dev, devices):
    columns_here = span_ids.shape[0]
    ordering = jnp.argsort(span_ids, stable=True)
    ranked = span_ids[ordering]
    starts = jnp.searchsorted(ranked, ranked, side="left")
    within = jnp.arange(columns_here, dtype=jnp.int32) - starts
    position = jnp.zeros((columns_here,), jnp.int32).at[ordering].set(within)
    owner = span_ids // per_dev
    local_span = span_ids % per_dev
    return local_span * (devices * capacity) + owner * capacity + position


def apply_blocks(received, inverses):
    applied = jnp.einsum("jab,qbjm->qajm", inverses, received, preferred_element_type=jnp.float32)
    return applied.astype(jnp.bfloat16)


def route(columns, span_ids, inverses, capacity, process):
    groups, levels, columns_here = columns.shape
    per_dev = inverses.shape[0]
    devices = lax.axis_size("elem")
    slot_of = slot_index(span_ids, capacity, per_dev, devices)
    outgoing = (
        jnp.zeros((groups, levels, per_dev * devices * capacity), jnp.bfloat16)
        .at[:, :, slot_of]
        .set(columns)
    )
    outgoing = outgoing.reshape(groups, levels, per_dev, devices * capacity)
    received = lax.all_to_all(outgoing, "elem", split_axis=3, concat_axis=3, tiled=True)
    returned = lax.all_to_all(process(received), "elem", split_axis=3, concat_axis=3, tiled=True)
    returned = returned.reshape(returned.shape[0], returned.shape[1], per_dev * devices * capacity)
    return returned[:, :, slot_of]


def body(tracers, wind_x, wind_y, span_of, inverses):
    derivative = derivative_table()
    groups, half_levels, width_x, width_y = tracers.shape
    table_x = jnp.asarray(np.kron(np.eye(width_x // NP), derivative).astype(np.float32))
    table_y = jnp.asarray(np.kron(np.eye(width_y // NP), derivative).astype(np.float32))
    winds_x = wind_x.astype(jnp.float32)[None]
    winds_y = wind_y.astype(jnp.float32)[None]
    field_state = tracers.astype(jnp.float32)
    for substep in range(NSUB):
        field_state = advance(field_state, table_x, table_y, winds_x, winds_y)
    dynamics = field_state.astype(jnp.bfloat16).reshape(groups, half_levels, width_x * width_y)
    span_ids = span_of[:, 0]
    per_dev = inverses.shape[0]
    devices = lax.axis_size("elem")
    capacity = max(2, 2 * dynamics.shape[2] // (per_dev * devices))

    def solve_levels(received):
        return apply_blocks(received, inverses)

    result = level_return(route(tracer_split(dynamics), span_ids, inverses, capacity, solve_levels))
    return result.reshape(groups, half_levels, width_x, width_y)


def solution(mesh):
    return jax.shard_map(
        body,
        mesh=mesh,
        in_specs=(
            P(None, "lev", "elem", None),
            P("lev", "elem", None),
            P("lev", "elem", None),
            P("elem", None),
            P("elem", None, None),
        ),
        out_specs=P(None, "lev", "elem", None),
        check_vma=False,
    )
```

profile of v0, /device:TPU:1, one launch (start us, length us, event | category | flops | bytes accessed | tf_op | source)
XLA Modules:
  0.0 917.7 jit_solution(16013802395696185528)
XLA Ops:
  14.3 11.1 %collective-permute-start = (f32[40,36,1,128]{3,2,1,0:T(1,128)S(1)}, f32[40,36,1,128]{3,2,1,0:T(1,128)S(1)}, u32[]{:S(2)}, u32[]{:S(2)}) collective-permute-start(f32[40,36,1,128]{3,2,1,0:T(1,128)S(1)} %get-tuple-element.112), channel_id=1, source_target_pairs={{2,0},{4,2},{6,4},{8,6},{10,8},{12,10},{14,12},{16,14},{18,16},{20... | collective-permute-start | bytes 2211848 | tf_op jit(solution)/shard_map/ppermute | solution.py:22
  34.6 6.0 collective-permute-done
  40.6 7.5 collective-permute-done.1
  48.1 9.2 %fusion.11 = f32[40,36,8,128]{3,2,1,0:T(8,128)S(1)} fusion(f32[40,36,8,128]{3,2,1,0:T(8,128)} %copy-done.3, f32[40,36,1,128]{3,2,1,0:T(1,128)S(1)} %collective-permute-done.1, f32[40,36,1,128]{3,2,1,0:T(1,128)S(1)} %collective-permute-done, pred[8]{0:T(512)(128)(4,1)S(1)} %get-tuple-element.116, pred[8]{0:T(512)(128)(4,1)S(1)} %get-tuple-element.117), kind=kLoop, calls=%fused_computation.23 | loop fusion | flops 11796480 | bytes 13271056 | tf_op jit(solution)/shard_map/jit(_where)/select_n | solution.py:55
  57.3 6.6 fusion.45
  63.9 6.6 fusion.46
  70.4 15.8 %fusion.15 = f32[40,36,8,128]{3,2,1,0:T(8,128)S(1)} fusion(f32[40,36,8,1]{3,2,1,0:T(8,128)} %get-tuple-element.109, f32[40,36,8,127]{3,2,1,0:T(8,128)} %get-tuple-element.111, f32[40,36,8,127]{3,2,1,0:T(8,128)} %get-tuple-element.110, f32[40,36,8,1]{3,2,1,0:T(8,128)} %get-tuple-element.108, pred[128]{0:T(512)(128)(4,1)S(1)} %get-tuple-element.118, ...), kind=kLoop, calls=%fused_computation.29 | loop fusion | flops 23592960 | bytes 25067792 | tf_op jit(solution)/shard_map/jit(_where)/select_n | solution.py:63
  86.2 5.1 fusion.49
  91.3 7.9 fusion.25
  104.4 50.7 %while.25 = (s32[]{:T(128)}, u32[1024]{0:T(1024)S(1)}, u32[1024]{0:T(1024)S(1)}, s32[1024]{0:T(1024)S(1)}, s32[]{:T(128)}, /*index=5*/s32[]{:T(128)}, s32[]{}) while((s32[]{:T(128)}, u32[1024]{0:T(1024)S(1)}, u32[1024]{0:T(1024)S(1)}, s32[1024]{0:T(1024)S(1)}, s32[]{:T(128)}, /*index=5*/s32[]{:T(128)}, s32[]{}) %tuple.46), condition=%wide.region_2.3_spmd.clone, body=%wide.region_1.2_spmd.clone.sunk | while | flops 19460 | bytes 67685 | solution.py:82
  109.0 4.5 gather_fusion
  113.6 4.5 gather_fusion
  118.2 4.5 gather_fusion
  122.8 4.5 gather_fusion
  127.4 4.5 gather_fusion
  159.4 9.2 %fusion.5 = f32[40,36,8,128]{3,2,1,0:T(8,128)S(1)} fusion(f32[40,36,8,128]{3,2,1,0:T(8,128)} %copy-done.2, f32[40,36,1,128]{3,2,1,0:T(1,128)S(1)} %collective-permute-done.3, f32[40,36,1,128]{3,2,1,0:T(1,128)S(1)} %collective-permute-done.2, pred[8]{0:T(512)(128)(4,1)S(1)} %get-tuple-element.116, pred[8]{0:T(512)(128)(4,1)S(1)} %get-tuple-element.117), kind=kLoop, calls=%fused_computation.15 | loop fusion | flops 11796480 | bytes 13271056 | tf_op jit(solution)/shard_map/jit(_where)/select_n | solution.py:55
  168.7 6.6 fusion.42
  175.3 6.6 fusion.43
  181.8 16.8 %fusion.20 = bf16[40,36,8,128]{3,2,1,0:T(8,128)(2,1)} fusion(f32[40,36,8,1]{3,2,1,0:T(8,128)} %get-tuple-element.103, f32[40,36,8,127]{3,2,1,0:T(8,128)} %get-tuple-element.105, f32[40,36,8,127]{3,2,1,0:T(8,128)} %get-tuple-element.104, f32[40,36,8,1]{3,2,1,0:T(8,128)} %get-tuple-element.102, pred[128]{0:T(512)(128)(4,1)S(1)} %get-tuple-element.118, ...), kind=kLoop, calls=%fused_computation.36 | loop fusion | flops 25067520 | bytes 22118672 | tf_op jit(solution)/shard_map/convert_element_type | solution.py:122
  202.9 8.4 all_to_all.43
  214.5 7.9 copy.48
  222.3 5.7 broadcast_in_dim.70
  228.1 127.3 %scatter_fusion = bf16[20,72,2048]{1,0,2:T(8,128)(2,1)} fusion(bf16[20,72,2048]{1,0,2:T(8,128)(2,1)} %broadcast_in_dim.70, s32[1024]{0:T(1024)S(1)} %get-tuple-element.101, bf16[1024,20,72]{2,1,0:T(8,128)(2,1)} %copy.48), kind=kCustom, calls=%fused_computation.4 | custom fusion | bytes 8851456 | tf_op jit(solution)/shard_map/scatter | solution.py:103
  355.4 11.3 %copy.50 = bf16[20,72,8,256]{1,2,0,3:T(8,128)(2,1)S(1)} copy(bf16[20,72,8,256]{1,0,3,2:T(8,128)(2,1)} %bitcast.58) | data formatting | bytes 11796480 | tf_op jit(solution)/shard_map/reshape | solution.py:105
  366.7 241.0 %all_to_all.44 = bf16[20,72,8,256]{1,2,0,3:T(8,128)(2,1)} all-to-all(bf16[20,72,8,256]{1,2,0,3:T(8,128)(2,1)S(1)} %copy.50), channel_id=1, replica_groups=mesh['elem'=128,'lev'=2] {'elem'}, dimensions={3} | all-to-all | bytes 11796480 | tf_op jit(solution)/shard_map/all_to_all | solution.py:106
  607.7 13.1 %convert_bitcast_fusion = bf16[20,72,8,256]{3,1,0,2:T(8,128)(2,1)} fusion(bf16[20,72,8,256]{1,2,0,3:T(8,128)(2,1)} %all_to_all.44, bf16[8,72,72]{2,1,0:T(8,128)(2,1)S(1)} %copy-done), kind=kOutput, calls=%fused_computation.49 | convolution fusion | flops 427622400 | bytes 11879424 | tf_op jit(solution)/shard_map/jab,qbjm->qajm/dot_general | solution.py:91
  620.7 13.1 %copy.52 = bf16[20,72,8,256]{1,2,0,3:T(8,128)(2,1)} copy(bf16[20,72,8,256]{3,1,0,2:T(8,128)(2,1)} %convert_bitcast_fusion) | data formatting | bytes 11796480 | tf_op jit(solution)/shard_map/convert_element_type | solution.py:92
  633.8 237.4 %all_to_all.45 = bf16[20,72,8,256]{1,2,0,3:T(8,128)(2,1)S(1)} all-to-all(bf16[20,72,8,256]{1,2,0,3:T(8,128)(2,1)} %copy.52), channel_id=1, replica_groups=mesh['elem'=128,'lev'=2] {'elem'}, dimensions={3} | all-to-all | bytes 11796480 | tf_op jit(solution)/shard_map/all_to_all | solution.py:107
  871.2 6.6 copy.64
  877.8 13.8 %gather_fusion.2 = bf16[1024,20,72]{2,1,0:T(8,128)(2,1)} fusion(bf16[20,72,2048]{1,0,2:T(8,128)(2,1)} %bitcast.59, s32[1024]{0:T(1024)S(1)} %get-tuple-element.100), kind=kCustom, calls=%fused_computation.2 | custom fusion | bytes 5902336 | tf_op jit(solution)/shard_map/gather | solution.py:109
  891.5 8.9 copy.55
  900.5 11.8 %all_to_all.46 = bf16[20,72,1024]{2,0,1:T(8,128)(2,1)S(1)} all-to-all(bf16[20,72,1024]{2,0,1:T(8,128)(2,1)} %copy.55), channel_id=1, replica_groups=mesh['elem'=128,'lev'=2] {'lev'}, dimensions={1} | all-to-all | bytes 5898240 | tf_op jit(solution)/shard_map/all_to_all | solution.py:75
  (91 shorter events, 72.7 us)
Async XLA Ops:
  0.0 607.7 %copy-start = (bf16[8,72,72]{2,1,0:T(8,128)(2,1)S(1)}, bf16[8,72,72]{2,1,0:T(8,128)(2,1)}, u32[]{:S(2)}) copy-start(bf16[8,72,72]{2,1,0:T(8,128)(2,1)} %param.13) | copy-start | bytes 248836
  0.0 6.4 copy-start.6
  0.0 6.4 copy-start.4
  6.5 19.2 %copy-start.1 = (s32[1024,1]{0,1:T(1,128)S(1)}, s32[1024,1]{0,1:T(1,128)}, u32[]{:S(2)}) copy-start(s32[1024,1]{0,1:T(1,128)} %param.12) | copy-start | bytes 12292
  10.8 2.5 copy-start.3
  14.3 26.3 %collective-permute-start = (f32[40,36,1,128]{3,2,1,0:T(1,128)S(1)}, f32[40,36,1,128]{3,2,1,0:T(1,128)S(1)}, u32[]{:S(2)}, u32[]{:S(2)}) collective-permute-start(f32[40,36,1,128]{3,2,1,0:T(1,128)S(1)} %get-tuple-element.112), channel_id=1, source_target_pairs={{2,0},{4,2},{6,4},{8,6},{10,8},{12,10},{14,12},{16,14},{18,16},{20... | collective-permute-start | bytes 2211848 | tf_op jit(solution)/shard_map/ppermute | solution.py:22
  25.4 22.7 %collective-permute-start.1 = (f32[40,36,1,128]{3,2,1,0:T(1,128)S(1)}, f32[40,36,1,128]{3,2,1,0:T(1,128)S(1)}, u32[]{:S(2)}, u32[]{:S(2)}) collective-permute-start(f32[40,36,1,128]{3,2,1,0:T(1,128)S(1)} %get-tuple-element.113), channel_id=1, source_target_pairs={{0,2},{2,4},{4,6},{6,8},{8,10},{10,12},{12,14},{14,16},{16,18},{18... | collective-permute-start | bytes 2211848 | tf_op jit(solution)/shard_map/ppermute | solution.py:21
  70.4 15.8 %copy-start.5 = (f32[128,128,1,1]{1,0,3,2:T(8,128)S(1)}, f32[128,128,1,1]{1,0,3,2:T(8,128)}, u32[]{:S(2)}) copy-start(f32[128,128,1,1]{1,0,3,2:T(8,128)} %constant.120) | copy-start | bytes 196612
  99.2 2.5 copy-start.2
  102.8 56.6 %collective-permute-start.2 = (f32[40,36,1,128]{3,2,1,0:T(1,128)S(1)}, f32[40,36,1,128]{3,2,1,0:T(1,128)S(1)}, u32[]{:S(2)}, u32[]{:S(2)}) collective-permute-start(f32[40,36,1,128]{3,2,1,0:T(1,128)S(1)} %get-tuple-element.106), channel_id=1, source_target_pairs={{2,0},{4,2},{6,4},{8,6},{10,8},{12,10},{14,12},{16,14},{18,16},{20... | collective-permute-start | bytes 2211848 | tf_op jit(solution)/shard_map/ppermute | solution.py:22
  103.0 56.4 %collective-permute-start.3 = (f32[40,36,1,128]{3,2,1,0:T(1,128)S(1)}, f32[40,36,1,128]{3,2,1,0:T(1,128)S(1)}, u32[]{:S(2)}, u32[]{:S(2)}) collective-permute-start(f32[40,36,1,128]{3,2,1,0:T(1,128)S(1)} %get-tuple-element.107), channel_id=1, source_target_pairs={{0,2},{2,4},{4,6},{6,8},{8,10},{10,12},{12,14},{14,16},{16,18},{18... | collective-permute-start | bytes 2211848 | tf_op jit(solution)/shard_map/ppermute | solution.py:21
where the time goes:
time: 928 us; the launch traced here: 918 us
  blocking collectives  499 us (54%)
  local copies, waits for them, and re-layouts  299 us (32%)
  other arithmetic  57.7 us (6%)
  matrix products  34.8 us (4%)
  waiting for transfers between devices  13.5 us (1%)
  starting transfers between devices  12.9 us (1%)
    all_to_all x1, blocking collectives, route(): lax.all_to_all(outgoing, 'elem', split_axis=3, concat_axis=3, tiled=True)  241 us
    all_to_all x1, blocking collectives, route(): lax.all_to_all(process(received), 'elem', split_axis=3, concat_axis=3, ti...  237 us
    scatter x1, local copies, waits for them, and re-layouts, route(): outgoing = jnp.zeros((groups, levels, per_dev * devices * capacity), jnp....  127 us
    gather x11, local copies, waits for them, and re-layouts, slot_index(): starts = jnp.searchsorted(ranked, ranked, side='left')  49.8 us
    slice x4, local copies, waits for them, and re-layouts, advance(): preceding = jnp.roll(mixed_x, 1, axis=3)  26.3 us
    gather x2, local copies, waits for them, and re-layouts, route(): return returned[:, :, slot_of]  22.7 us
  transfers between devices with their start and end apart: 4, of which 2 were waited for; matrix products, arithmetic and copies ran while one was open for 7% of the time, Pallas kernels for 0%

commit v1 on v0

v1 whole, which is shorter than its diff:
```python
import jax
import jax.numpy as jnp
import numpy as np
from jax import lax
from jax.experimental import pallas as pl
from jax.experimental.pallas import tpu as pltpu
from jax.sharding import PartitionSpec as P

NP = 4
TIME_STEP = 0.08
NY_CHIPS, NX_CHIPS, NZ_CHIPS = 4, 4, 8
CHUNKS = 2
F32, BF16 = jnp.float32, jnp.bfloat16


def derivative_table():
    nodes = np.array([-1.0, -1.0 / np.sqrt(5.0), 1.0 / np.sqrt(5.0), 1.0])
    table = np.zeros((NP, NP))
    for i in range(NP):
        for k in range(NP):
            if i == k:
                table[i, k] = sum(1.0 / (nodes[i] - nodes[m]) for m in range(NP) if m != i)
            else:
                top = np.prod([nodes[i] - nodes[m] for m in range(NP) if m != k and m != i])
                table[i, k] = top / np.prod([nodes[k] - nodes[m] for m in range(NP) if m != k])
    return table


D = derivative_table()
D = [[float(D[i, k]) for k in range(NP)] for i in range(NP)]


def table_y(width):
    full = np.kron(np.eye(width // NP), np.array(D)).T.astype(np.float32)
    hi = full.astype(jnp.bfloat16)
    lo = (full - hi.astype(np.float32)).astype(jnp.bfloat16)
    first = np.concatenate([hi, lo], axis=0)
    zero = np.zeros_like(lo)
    second = np.concatenate(
        [np.concatenate([hi, lo], axis=1), np.concatenate([hi, zero], axis=1)], axis=0
    )
    return jnp.asarray(first), jnp.asarray(second)


def grad_x(s0, s1, s2, s3):
    m, n = s3 - s0, s2 - s1
    e = (s0 + s3) - (s1 + s2)
    a = 0.5 * (D[3][3] + D[0][3])
    b = 0.5 * (D[0][1] + D[3][1])
    u = a * m - b * n
    v = (0.5 * (D[1][3] + D[2][3])) * m + (0.5 * (D[1][2] + D[2][2])) * n
    w = (0.5 * (D[3][3] - D[0][3])) * e
    z = (0.5 * (D[2][3] - D[1][3])) * e
    return [u - w, v - z, v + z, u + w]


def mean_y(value, last, inner):
    width = value.shape[1]
    ahead = pltpu.roll(value, width - 1, axis=1)
    behind = pltpu.roll(value, 1, axis=1)
    return jnp.where(inner, value, 0.5 * (value + jnp.where(last, ahead, behind)))


def node_masks(shape):
    node = lax.broadcasted_iota(jnp.int32, shape, 1) % NP
    return node == NP - 1, (node == 1) | (node == 2)


def first_kernel(levels, t_ref, wx_ref, wy_ref, d_ref, st_ref, dn_ref, up_ref, scr):
    groups, width_x, width_y = t_ref.shape[0], t_ref.shape[2], t_ref.shape[3]
    last, inner = node_masks((groups, width_y))

    @pl.loop(0, levels)
    def _(l):
        scr[...] = t_ref[:, l].astype(F32).reshape(groups * width_x, width_y)
        s = [scr[pl.ds(x, groups, stride=width_x), :] for x in range(width_x)]
        wx = wx_ref[l].astype(F32) * TIME_STEP
        wy = wy_ref[l].astype(F32) * TIME_STEP
        flat = jnp.concatenate(s, axis=0).astype(BF16)
        gy = jnp.dot(
            jnp.concatenate([flat, flat], axis=1), d_ref[...], preferred_element_type=F32
        )
        gx = grad_x(*s[:4]) + grad_x(*s[4:])
        adv = [
            s[x]
            - (wx[x : x + 1] * gx[x] + wy[x : x + 1] * gy[x * groups : (x + 1) * groups])
            for x in range(width_x)
        ]
        middle = mean_y(0.5 * (adv[3] + adv[4]), last, inner)
        st = [adv[0], None, None, middle, middle, None, None, adv[7]]
        for x in (1, 2, 5, 6):
            st[x] = mean_y(adv[x], last, inner)
        for x in range(width_x):
            st_ref[l, x] = st[x]
        part = D[0][1] * st[1] + D[0][2] * st[2] + D[0][3] * st[3]
        dn_ref[l, 0] = adv[0].astype(BF16)
        dn_ref[l, 1] = (-wx[0:1] * part).astype(BF16)
        part = D[3][0] * st[4] + D[3][1] * st[5] + D[3][2] * st[6]
        up_ref[l, 0] = adv[7].astype(BF16)
        up_ref[l, 1] = (-wx[7:8] * part).astype(BF16)


def second_kernel(
    levels, st_ref, left_ref, right_ref, wx_ref, wy_ref, wl_ref, wr_ref, d_ref, out_ref
):
    width_x, groups, width_y = st_ref.shape[1:]
    last, inner = node_masks((groups, width_y))

    @pl.loop(0, levels)
    def _(l):
        s = [None] + [st_ref[l, x] for x in range(1, 7)] + [None]
        s[0] = mean_y(0.5 * (st_ref[l, 0] + left_ref[l, 0].astype(F32)), last, inner)
        s[7] = mean_y(0.5 * (st_ref[l, 7] + right_ref[l, 0].astype(F32)), last, inner)
        wx = wx_ref[l].astype(F32) * TIME_STEP
        wy = wy_ref[l].astype(F32) * TIME_STEP
        wl = wl_ref[l].astype(F32) * TIME_STEP
        wr = wr_ref[l].astype(F32) * TIME_STEP
        flat = jnp.concatenate(s, axis=0)
        hi = flat.astype(BF16)
        lo = (flat - hi.astype(F32)).astype(BF16)
        both = jnp.dot(
            jnp.concatenate([hi, lo], axis=1), d_ref[...], preferred_element_type=F32
        )
        gy = both[:, :width_y] + both[:, width_y:]
        gys = [gy[x * groups : (x + 1) * groups] for x in range(width_x)]
        gx = grad_x(*s[:4]) + grad_x(*s[4:])
        adv = [
            s[x] - (wx[x : x + 1] * gx[x] + wy[x : x + 1] * gys[x]) for x in range(width_x)
        ]
        before = (
            s[0]
            - ((wl[0:1] * D[3][3]) * s[0] + wl[1:2] * gys[0])
            + left_ref[l, 1].astype(F32)
        )
        after = (
            s[7]
            - ((wr[0:1] * D[0][0]) * s[7] + wr[1:2] * gys[7])
            + right_ref[l, 1].astype(F32)
        )
        middle = 0.5 * (adv[3] + adv[4])
        adv[0] = 0.5 * (before + adv[0])
        adv[7] = 0.5 * (adv[7] + after)
        adv[3] = middle
        for x in range(width_x):
            if x != 4:
                done = mean_y(adv[x], last, inner).astype(BF16)
                out_ref[l, x] = done
                if x == 3:
                    out_ref[l, 4] = done


def first_part(tracers, wind_x, wind_y, table, start, count):
    groups, _, width_x, width_y = tracers.shape
    step = 3
    skip = start // step
    spec_w = pl.BlockSpec((step, width_x, width_y), lambda i: (i + skip, 0, 0))
    spec_m = pl.BlockSpec((step, 2, groups, width_y), lambda i: (i, 0, 0, 0))
    return pl.pallas_call(
        lambda *refs: first_kernel(step, *refs),
        grid=(count // step,),
        in_specs=[
            pl.BlockSpec((groups, step, width_x, width_y), lambda i: (0, i + skip, 0, 0)),
            spec_w,
            spec_w,
            pl.BlockSpec(table.shape, lambda i: (0, 0)),
        ],
        out_specs=[
            pl.BlockSpec((step, width_x, groups, width_y), lambda i: (i, 0, 0, 0)),
            spec_m,
            spec_m,
        ],
        out_shape=[
            jax.ShapeDtypeStruct((count, width_x, groups, width_y), F32),
            jax.ShapeDtypeStruct((count, 2, groups, width_y), BF16),
            jax.ShapeDtypeStruct((count, 2, groups, width_y), BF16),
        ],
        scratch_shapes=[pltpu.VMEM((groups * width_x, width_y), F32)],
        compiler_params=pltpu.CompilerParams(vmem_limit_bytes=24 << 20),
        cost_estimate=pl.CostEstimate(
            flops=40 * count * width_x * groups * width_y,
            bytes_accessed=8 * count * width_x * groups * width_y,
            transcendentals=0,
        ),
        name="transport_first",
    )(tracers, wind_x, wind_y, table)


def second_part(state, left, right, wind_x, wind_y, wind_l, wind_r, table, start):
    count, width_x, groups, width_y = state.shape
    step = 3
    skip = start // step
    spec_s = pl.BlockSpec((step, width_x, groups, width_y), lambda i: (i, 0, 0, 0))
    spec_m = pl.BlockSpec((step, 2, groups, width_y), lambda i: (i, 0, 0, 0))
    spec_w = pl.BlockSpec((step, width_x, width_y), lambda i: (i + skip, 0, 0))
    spec_n = pl.BlockSpec((step, 2, width_y), lambda i: (i + skip, 0, 0))
    return pl.pallas_call(
        lambda *refs: second_kernel(step, *refs),
        grid=(count // step,),
        in_specs=[
            spec_s, spec_m, spec_m, spec_w, spec_w, spec_n, spec_n,
            pl.BlockSpec(table.shape, lambda i: (0, 0)),
        ],
        out_specs=spec_s,
        out_shape=jax.ShapeDtypeStruct(state.shape, BF16),
        compiler_params=pltpu.CompilerParams(vmem_limit_bytes=24 << 20),
        cost_estimate=pl.CostEstimate(
            flops=40 * count * width_x * groups * width_y,
            bytes_accessed=8 * count * width_x * groups * width_y,
            transcendentals=0,
        ),
        name="transport_second",
    )(state, left, right, wind_x, wind_y, wind_l, wind_r, table)


A_STEP = 6


def solve_kernel(n_fields, half_rows, pos_ref, *refs):
    fields = refs[:n_fields]
    pieces = refs[n_fields : n_fields + 10]
    out_ref = refs[n_fields + 10]
    value, choice, chosen, result = refs[n_fields + 11 :]
    width_x, groups, width_y = value.shape[1:]
    levels = value.shape[0]
    step = pl.program_id(0)
    half = pl.num_programs(0) // 2

    @pl.when(step == 0)
    def _():
        base = 0
        for field in fields:
            count = field.shape[0]

            @pl.loop(0, count)
            def _(l, base=base, field=field):
                for x in range(width_x):
                    value[base + l, x] = field[l, x].astype(F32)

            base += count
        spans = choice.shape[0]
        for x in range(width_x):
            for k in range(spans // 128):
                row = lax.broadcasted_iota(jnp.int32, (128, width_y), 0) + k * 128
                hit = row == pos_ref[x : x + 1, :]
                choice[k * 128 : (k + 1) * 128, x * width_y : (x + 1) * width_y] = (
                    jnp.where(hit, 1.0, 0.0).astype(BF16)
                )

    early = step < half
    blocks = []
    for group in range(2):
        a, b, lo, hi, c = pieces[group * 5 : group * 5 + 5]
        blocks += [a[...], b[...], jnp.where(early, lo[...], hi[...]), c[...]]
    matrices = jnp.concatenate(blocks, axis=1)
    for x in range(0, width_x, 2):
        cols = slice(x * width_y, (x + 2) * width_y)
        chosen[:, cols] = jnp.dot(matrices, choice[:, cols], preferred_element_type=F32)

    @pl.loop(0, width_x)
    def _(x):
        lanes = pl.ds(pl.multiple_of(x * width_y, width_y), width_y)
        for first in range(0, A_STEP, 3):
            total = [jnp.zeros((groups, width_y), F32)] * 3
            for b in range(levels):
                levels_b = value[b, x]
                for i in range(3):
                    row = (first + i) * levels + b
                    total[i] = total[i] + chosen[row : row + 1, lanes] * levels_b
            for i in range(3):
                result[first + i, pl.ds(x, groups, stride=width_x), :] = total[i]

    for a in range(A_STEP):
        out_ref[:, a] = result[a].reshape(groups, width_x, width_y).astype(BF16)


def solve(fields, pieces, position, groups, levels_out, width_x, width_y):
    levels = sum(f.shape[0] for f in fields)
    rows = A_STEP * levels
    steps = levels_out // A_STEP
    half = steps // 2
    full = pl.BlockSpec((rows, 128), lambda i: (i, 0))
    low = pl.BlockSpec((rows, 128), lambda i: (jnp.minimum(i, half - 1), 0))
    high = pl.BlockSpec((rows, 128), lambda i: (jnp.maximum(i - half, 0), 0))
    spans = 1024
    return pl.pallas_call(
        lambda *refs: solve_kernel(len(fields), rows * half, *refs),
        grid=(steps,),
        in_specs=[pl.BlockSpec(position.shape, lambda i: (0, 0))]
        + [pl.BlockSpec(f.shape, lambda i: (0, 0, 0, 0)) for f in fields]
        + [full, full, low, high, full] * 2,
        out_specs=pl.BlockSpec((groups, A_STEP, width_x, width_y), lambda i: (0, i, 0, 0)),
        out_shape=jax.ShapeDtypeStruct((groups, levels_out, width_x, width_y), BF16),
        scratch_shapes=[
            pltpu.VMEM((levels, width_x, groups, width_y), F32),
            pltpu.VMEM((spans, width_x * width_y), BF16),
            pltpu.VMEM((rows, width_x * width_y), F32),
            pltpu.VMEM((A_STEP, groups * width_x, width_y), F32),
        ],
        compiler_params=pltpu.CompilerParams(vmem_limit_bytes=48 << 20),
        cost_estimate=pl.CostEstimate(
            flops=2 * levels_out * levels * groups * width_x * width_y,
            bytes_accessed=12 << 20,
            transcendentals=0,
        ),
        name="solve_columns",
    )(position, *fields, *pieces)


def elem_index(y, x, z):
    return (y % NY_CHIPS * NX_CHIPS + x % NX_CHIPS) * NZ_CHIPS + z % NZ_CHIPS


def fetch(value, dy=0, dx=0, dz=0):
    pairs = [
        (elem_index(y + dy, x + dx, z + dz), elem_index(y, x, z))
        for y in range(NY_CHIPS)
        for x in range(NX_CHIPS)
        for z in range(NZ_CHIPS)
    ]
    return lax.ppermute(value, "elem", pairs)


def ring_of_four(value, axis, cut):
    ahead = fetch(value, **{axis: 1})
    behind = fetch(value, **{axis: -1})
    first = fetch(ahead[:cut], **{axis: 1})
    second = fetch(behind[cut:], **{axis: -1})
    return [value, ahead, first, second, behind]


def gather_matrices(rows):
    entries = rows.shape[1]
    cut = entries // 2
    near = [rows] + [fetch(rows, dz=d) for d in range(1, NZ_CHIPS)]
    pieces = []
    for group, (one, two) in enumerate((("dx", "dy"), ("dy", "dx"))):
        part = jnp.concatenate(near[group * 4 : group * 4 + 4], axis=0)
        value, ahead, first, second, behind = ring_of_four(part, one, part.shape[0] // 2)
        part = jnp.concatenate([value, ahead, first, second, behind], axis=0)
        pieces += ring_of_four(part.T, two, cut)
    return pieces


def span_position(span_ids, per_dev):
    here = lax.axis_index("elem")
    owner, local = span_ids // per_dev, span_ids % per_dev
    dz = (owner % NZ_CHIPS - here % NZ_CHIPS) % NZ_CHIPS
    dx = (owner // NZ_CHIPS % NX_CHIPS - here // NZ_CHIPS % NX_CHIPS) % NX_CHIPS
    dy = (owner // (NZ_CHIPS * NX_CHIPS) - here // (NZ_CHIPS * NX_CHIPS)) % NY_CHIPS
    inside = (dz % 4) * per_dev + local
    return jnp.where(
        dz < 4, dy * 128 + dx * 32 + inside, 512 + dx * 128 + dy * 32 + inside
    ).astype(jnp.int32)


def body(tracers, wind_x, wind_y, span_of, inverses):
    groups, half_levels, width_x, width_y = tracers.shape
    per_dev = inverses.shape[0]
    first_table, second_table = table_y(width_y)
    size = lax.axis_size("elem")
    up = [(i, (i + 1) % size) for i in range(size)]
    down = [(j, i) for i, j in up]
    lev = lax.axis_index("lev")

    mine = lax.dynamic_slice_in_dim(inverses, lev * half_levels, half_levels, 1)
    own = lax.dynamic_slice_in_dim(mine, lev * half_levels, half_levels, 2)
    other = lax.dynamic_slice_in_dim(mine, (1 - lev) * half_levels, half_levels, 2)
    rows = jnp.concatenate([own, other], axis=2).reshape(per_dev, -1)
    pieces = gather_matrices(rows)
    position = span_position(span_of[:, 0], per_dev).reshape(width_x, width_y)

    wind_l = lax.ppermute(jnp.stack([wind_x[:, -1], wind_y[:, -1]], 1), "elem", up)
    wind_r = lax.ppermute(jnp.stack([wind_x[:, 0], wind_y[:, 0]], 1), "elem", down)

    count = half_levels // CHUNKS
    firsts = [
        first_part(tracers, wind_x, wind_y, first_table, i * count, count)
        for i in range(CHUNKS)
    ]
    own_fields, other_fields = [], []
    for i, (state, to_left, to_right) in enumerate(firsts):
        left = lax.ppermute(to_right, "elem", up)
        right = lax.ppermute(to_left, "elem", down)
        field = second_part(
            state, left, right, wind_x, wind_y, wind_l, wind_r, second_table, i * count
        )
        own_fields.append(field)
        other_fields.append(lax.ppermute(field, "lev", [(0, 1), (1, 0)]))
    return solve(
        own_fields + other_fields, pieces, position, groups, half_levels, width_x, width_y
    )


def solution(mesh):
    return jax.shard_map(
        body,
        mesh=mesh,
        in_specs=(
            P(None, "lev", "elem", None),
            P("lev", "elem", None),
            P("lev", "elem", None),
            P("elem", None),
            P("elem", None, None),
        ),
        out_specs=P(None, "lev", "elem", None),
        check_vma=False,
    )
```

time: 928 us -> 243 us (0.26)
  blocking collectives: 499 us -> 0 us
  local copies, waits for them, and re-layouts: 299 us -> 65.7 us
  Pallas kernels: 0 us -> 77 us
  other arithmetic: 57.7 us -> 1.03 us
  starting transfers between devices: 12.9 us -> 64.1 us
  matrix products: 34.8 us -> 0 us
  waiting for transfers between devices: 13.5 us -> 30.1 us
    all_to_all x4 -> x0, blocking collectives: 499 us -> none  [the longest x1 241 us: route(): lax.all_to_all(outgoing, 'elem', split_axis=3, concat_axis=3, tiled=True)]
    scatter x2 -> x0, local copies, waits for them, and re-layouts: 132 us -> none  [the longest x1 127 us: route(): outgoing = jnp.zeros((groups, levels, per_dev * devices * capacity), jnp....]
    gather x14 -> x0, local copies, waits for them, and re-layouts: 77 us -> none  [the longest x11 49.8 us: slot_index(): starts = jnp.searchsorted(ranked, ranked, side='left')]
    pallas_call x0 -> x5, Pallas kernels: none -> 77 us  [the longest x1 51.9 us: solve(): pl.pallas_call(lambda *refs: solve_kernel(len(fields), rows * half, *refs...]
    ppermute x4 -> x31, starting transfers between devices: 12.9 us -> 64.1 us  [the longest x23 38.7 us: fetch(): return lax.ppermute(value, 'elem', pairs)]
    dot_general x5 -> x0, matrix products: 34.8 us -> none  [the longest x1 13.1 us: apply_blocks(): jnp.einsum('jab,qbjm->qajm', inverses, received, preferred_element_type=j...]
    select_n x25 -> x1, other arithmetic: 34.5 us -> 0.04 us  [span_position(): jnp.where(dz < 4, dy * 128 + dx * 32 + inside, 512 + dx * 128 + dy * 32 +...]
    reshape x4 -> x1, local copies, waits for them, and re-layouts: 25.5 us -> 0.86 us  [body(): rows = jnp.concatenate([own, other], axis=2).reshape(per_dev, -1)]
  transfers between devices with their start and end apart: 4 -> 31, of which waited for: 2 -> 7; matrix products, arithmetic and copies ran while one was open for 7% -> 19% of each run, Pallas kernels for 0% -> 11%
where the time goes in v1:
time: 243 us; the launch traced here: 238 us
  Pallas kernels  77 us (32%)
  local copies, waits for them, and re-layouts  65.7 us (27%)
  starting transfers between devices  64.1 us (26%)
  waiting for transfers between devices  30.1 us (12%)
    pallas_call x1, Pallas kernels, solve(): pl.pallas_call(lambda *refs: solve_kernel(len(fields), rows * half, *refs...  51.9 us
    ppermute x23, starting transfers between devices, fetch(): return lax.ppermute(value, 'elem', pairs)  38.7 us
    ppermute x23, waiting for transfers between devices, fetch(): return lax.ppermute(value, 'elem', pairs)  30.1 us
    ppermute x15, local copies, waits for them, and re-layouts, fetch(): return lax.ppermute(value, 'elem', pairs)  23.3 us
    unnamed x63, local copies, waits for them, and re-layouts  21.6 us
    ppermute x2, starting transfers between devices, body(): right = lax.ppermute(to_left, 'elem', down)  13.8 us
    pallas_call x2, Pallas kernels, second_part(): pl.pallas_call(lambda *refs: second_kernel(step, *refs), grid=(count // s...  12.9 us
    pallas_call x2, Pallas kernels, first_part(): pl.pallas_call(lambda *refs: first_kernel(step, *refs), grid=(count // st...  12.2 us
  transfers between devices with their start and end apart: 31, of which 7 were waited for; matrix products, arithmetic and copies ran while one was open for 19% of the time, Pallas kernels for 11%

profile of v1, /device:TPU:1, one launch (start us, length us, event | category | flops | bytes accessed | tf_op | source)
XLA Modules:
  0.0 238.2 jit_solution(9173461308519230989)
XLA Ops:
  2.4 3.8 %collective-permute-start.21 = (bf16[8,2592]{1,0:T(8,128)(2,1)}, bf16[8,2592]{1,0:T(8,128)(2,1)S(1)}, u32[]{:S(2)}, u32[]{:S(2)}) collective-permute-start(bf16[8,2592]{1,0:T(8,128)(2,1)} %copy.10), channel_id=1, source_target_pairs={{12,0},{14,2},{0,4},{2,6},{4,8},{6,10},{8,12},{10,14},{28,16},{30,... | collective-permute-start | bytes 124424 | tf_op jit(solution)/shard_map/ppermute | solution.py:320
  6.2 4.7 %collective-permute-start.20 = (bf16[8,2592]{1,0:T(8,128)(2,1)}, bf16[8,2592]{1,0:T(8,128)(2,1)S(1)}, u32[]{:S(2)}, u32[]{:S(2)}) collective-permute-start(bf16[8,2592]{1,0:T(8,128)(2,1)} %copy.10), channel_id=1, source_target_pairs={{10,0},{12,2},{14,4},{0,6},{2,8},{4,10},{6,12},{8,14},{26,16},{28,... | collective-permute-start | bytes 124424 | tf_op jit(solution)/shard_map/ppermute | solution.py:320
  10.9 2.8 %collective-permute-start.9 = (bf16[8,2592]{1,0:T(8,128)(2,1)}, bf16[8,2592]{1,0:T(8,128)(2,1)S(1)}, u32[]{:S(2)}, u32[]{:S(2)}) collective-permute-start(bf16[8,2592]{1,0:T(8,128)(2,1)} %copy.10), channel_id=1, source_target_pairs={{4,0},{6,2},{8,4},{10,6},{12,8},{14,10},{0,12},{2,14},{20,16},{22,... | collective-permute-start | bytes 124424 | tf_op jit(solution)/shard_map/ppermute | solution.py:320
  13.7 1.9 collective-permute-start.8
  21.3 5.8 %transport_first.3 = (f32[18,8,40,128]{3,2,1,0:T(8,128)S(1)}, bf16[18,2,40,128]{3,2,1,0:T(8,128)(2,1)S(1)}, bf16[18,2,40,128]{3,2,1,0:T(8,128)(2,1)S(1)}) custom-call(bf16[40,36,8,128]{3,2,1,0:T(8,128)(2,1)S(1)} %copy-done, bf16[36,8,128]{2,1,0:T(8,128)(2,1)S(1)} %copy-done.12, bf16[36,8,128]{2,1,0:T(8,128)(2,1)S(1)} %copy-done.14, ...), custom_call_target="tpu_custom_call" | custom-call | flops 29491200 | bytes 5898240 | tf_op jit(solution)/shard_map/transport_first/pallas_call | solution.py:158
  28.6 6.5 %transport_first.2 = (f32[18,8,40,128]{3,2,1,0:T(8,128)S(1)}, bf16[18,2,40,128]{3,2,1,0:T(8,128)(2,1)}, bf16[18,2,40,128]{3,2,1,0:T(8,128)(2,1)}) custom-call(bf16[40,36,8,128]{3,2,1,0:T(8,128)(2,1)S(1)} %copy-done, bf16[36,8,128]{2,1,0:T(8,128)(2,1)S(1)} %copy-done.12, bf16[36,8,128]{2,1,0:T(8,128)(2,1)S(1)} %copy-done.14, bf16[256,128]{1,0:T(8,128)(2,1)S(1)} %copy-done.21), custom_call_target="tpu_custom_call" | custom-call | flops 29491200 | bytes 5898240 | tf_op jit(solution)/shard_map/transport_first/pallas_call | solution.py:158
  36.7 2.6 %collective-permute-start.19 = (bf16[8,2592]{1,0:T(8,128)(2,1)}, bf16[8,2592]{1,0:T(8,128)(2,1)S(1)}, u32[]{:S(2)}, u32[]{:S(2)}) collective-permute-start(bf16[8,2592]{1,0:T(8,128)(2,1)} %copy.10), channel_id=1, source_target_pairs={{8,0},{10,2},{12,4},{14,6},{0,8},{2,10},{4,12},{6,14},{24,16},{26,... | collective-permute-start | bytes 124424 | tf_op jit(solution)/shard_map/ppermute | solution.py:320
  43.8 2.5 %collective-permute-start.11 = (bf16[32,2592]{1,0:T(8,128)(2,1)S(1)}, bf16[32,2592]{1,0:T(8,128)(2,1)S(1)}, u32[]{:S(2)}, u32[]{:S(2)}) collective-permute-start(bf16[32,2592]{1,0:T(8,128)(2,1)S(1)} %pad_maximum_fusion), channel_id=1, source_target_pairs={{16,0},{18,2},{20,4},{22,6},{24,8},{26,10},{28,12},{30,14},{32,16}... | collective-permute-start | bytes 497672 | tf_op jit(solution)/shard_map/ppermute | solution.py:320
  48.1 3.9 %collective-permute-start.3 = (bf16[36,2,128]{2,1,0:T(2,128)(2,1)S(1)}, bf16[36,2,128]{2,1,0:T(2,128)(2,1)S(1)}, u32[]{:S(2)}, u32[]{:S(2)}) collective-permute-start(bf16[36,2,128]{2,1,0:T(2,128)(2,1)S(1)} %pad_maximum_fusion.3), channel_id=1, source_target_pairs={{2,0},{4,2},{6,4},{8,6},{10,8},{12,10},{14,12},{16,14},{18,16},{20... | collective-permute-start | bytes 55304 | tf_op jit(solution)/shard_map/ppermute | solution.py:373
  52.2 2.7 %collective-permute-start.12 = (bf16[16,2592]{1,0:T(8,128)(2,1)S(1)}, bf16[16,2592]{1,0:T(8,128)(2,1)S(1)}, u32[]{:S(2)}, u32[]{:S(2)}) collective-permute-start(bf16[16,2592]{1,0:T(8,128)(2,1)S(1)} %slice.48), channel_id=1, source_target_pairs={{16,0},{18,2},{20,4},{22,6},{24,8},{26,10},{28,12},{30,14},{32,16}... | collective-permute-start | bytes 248840 | tf_op jit(solution)/shard_map/ppermute | solution.py:320
  55.6 6.9 %collective-permute-start.5 = (bf16[18,2,40,128]{3,2,1,0:T(8,128)(2,1)S(1)}, bf16[18,2,40,128]{3,2,1,0:T(8,128)(2,1)S(1)}, u32[]{:S(2)}, u32[]{:S(2)}) collective-permute-start(bf16[18,2,40,128]{3,2,1,0:T(8,128)(2,1)S(1)} %get-tuple-element.16), channel_id=1, source_target_pairs={{2,0},{4,2},{6,4},{8,6},{10,8},{12,10},{14,12},{16,14},{18,16},{20... | collective-permute-start | bytes 1105928 | tf_op jit(solution)/shard_map/ppermute | solution.py:383
  63.8 6.9 %collective-permute-start.1 = (bf16[18,2,40,128]{3,2,1,0:T(8,128)(2,1)}, bf16[18,2,40,128]{3,2,1,0:T(8,128)(2,1)S(1)}, u32[]{:S(2)}, u32[]{:S(2)}) collective-permute-start(bf16[18,2,40,128]{3,2,1,0:T(8,128)(2,1)} %get-tuple-element.13), channel_id=1, source_target_pairs={{2,0},{4,2},{6,4},{8,6},{10,8},{12,10},{14,12},{16,14},{18,16},{20... | collective-permute-start | bytes 1105928 | tf_op jit(solution)/shard_map/ppermute | solution.py:383
  75.0 1.9 copy.16
  79.2 2.0 copy.18
  81.2 2.0 copy.19
  83.3 5.9 %concatenate.19 = bf16[128,2592]{0,1:T(8,128)(2,1)} concatenate(bf16[8,2592]{0,1:T(8,128)(2,1)S(1)} %bitcast.8, bf16[8,2592]{0,1:T(8,128)(2,1)} %copy.14, bf16[8,2592]{0,1:T(8,128)(2,1)} %copy.15, bf16[8,2592]{0,1:T(8,128)(2,1)} %copy.16, bf16[32,2592]{0,1:T(8,128)(2,1)} %copy.17, bf16[16,2592]{0,1:T(8,128)(2,1)} %copy.18, bf16[16,2592]{0,1:T(8,128)(2,1)} %copy.19, ...), dimensions={0} | concatenate | bytes 1327104 | tf_op jit(solution)/shard_map/concatenate | solution.py:339
  89.9 2.7 %collective-permute-start.23 = (bf16[32,2592]{1,0:T(8,128)(2,1)}, bf16[32,2592]{1,0:T(8,128)(2,1)S(1)}, u32[]{:S(2)}, u32[]{:S(2)}) collective-permute-start(bf16[32,2592]{1,0:T(8,128)(2,1)} %constant_dynamic-update-slice_fusion), channel_id=1, source_target_pairs={{64,0},{66,2},{68,4},{70,6},{72,8},{74,10},{76,12},{78,14},{80,16}... | collective-permute-start | bytes 497672 | tf_op jit(solution)/shard_map/ppermute | solution.py:320
  94.4 6.4 %transport_second.3.refs_2_ = bf16[18,8,40,128]{3,2,1,0:T(8,128)(2,1)S(1)} custom-call(f32[18,8,40,128]{3,2,1,0:T(8,128)S(1)} %copy-done.6, bf16[18,2,40,128]{3,2,1,0:T(8,128)(2,1)S(1)} %collective-permute-done.4.refs_1_, bf16[18,2,40,128]{3,2,1,0:T(8,128)(2,1)S(1)} %collective-permute-done.5.refs_2_, bf16[36,8,128]{2,1,0:T(8,128)(2,1)S(1)} %copy-done.13, ...), custom_call_target="tpu_custom_call" | custom-call | flops 29491200 | bytes 5898240 | tf_op jit(solution)/shard_map/transport_second/pallas_call | solution.py:196
  100.9 6.0 %collective-permute-start.7 = (bf16[18,8,40,128]{3,2,1,0:T(8,128)(2,1)S(1)}, bf16[18,8,40,128]{3,2,1,0:T(8,128)(2,1)}, u32[]{:S(2)}, u32[]{:S(2)}) collective-permute-start(bf16[18,8,40,128]{3,2,1,0:T(8,128)(2,1)S(1)} %transport_second.3.refs_2_), channel_id=1, source_target_pairs={{0,1},{1,0},{2,3},{3,2},{4,5},{5,4},{6,7},{7,6},{8,9},{9,8},{10,11... | collective-permute-start | bytes 4423688 | tf_op jit(solution)/shard_map/ppermute | solution.py:388
  110.4 6.4 %transport_second.2.refs_1_ = bf16[18,8,40,128]{3,2,1,0:T(8,128)(2,1)S(1)} custom-call(f32[18,8,40,128]{3,2,1,0:T(8,128)S(1)} %copy-done.4, bf16[18,2,40,128]{3,2,1,0:T(8,128)(2,1)S(1)} %copy-done.18, bf16[18,2,40,128]{3,2,1,0:T(8,128)(2,1)S(1)} %copy-done.20, bf16[36,8,128]{2,1,0:T(8,128)(2,1)S(1)} %copy-done.13, bf16[36,8,128]{2,1,0:T(8,128)(2,1)S(1)} %copy-done.15, ...), custom_call_target="tpu_custom_call" | custom-call | flops 29491200 | bytes 5898240 | tf_op jit(solution)/shard_map/transport_second/pallas_call | solution.py:196
  117.0 2.7 %collective-permute-start.15 = (bf16[2592,128]{1,0:T(8,128)(2,1)}, bf16[2592,128]{1,0:T(8,128)(2,1)}, u32[]{:S(2)}, u32[]{:S(2)}) collective-permute-start(bf16[2592,128]{1,0:T(8,128)(2,1)} %bitcast.2.refs_5_), channel_id=1, source_target_pairs={{64,0},{66,2},{68,4},{70,6},{72,8},{74,10},{76,12},{78,14},{80,16}... | collective-permute-start | bytes 1990664 | tf_op jit(solution)/shard_map/ppermute | solution.py:320
  119.7 4.3 %collective-permute-done.25 = bf16[32,2592]{1,0:T(8,128)(2,1)S(1)} collective-permute-done((bf16[32,2592]{1,0:T(8,128)(2,1)}, bf16[32,2592]{1,0:T(8,128)(2,1)S(1)}, u32[]{:S(2)}, u32[]{:S(2)}) %collective-permute-start.25) | collective-permute-done | bytes 165920 | tf_op jit(solution)/shard_map/ppermute | solution.py:320
  124.7 10.7 %collective-permute-done.24 = bf16[16,2592]{1,0:T(8,128)(2,1)S(1)} collective-permute-done((bf16[16,2592]{1,0:T(8,128)(2,1)S(1)}, bf16[16,2592]{1,0:T(8,128)(2,1)S(1)}, u32[]{:S(2)}, u32[]{:S(2)}) %collective-permute-start.24) | collective-permute-done | bytes 82976 | tf_op jit(solution)/shard_map/ppermute | solution.py:320
  144.8 2.0 copy.31
  146.8 6.0 %concatenate.21 = bf16[128,2592]{0,1:T(8,128)(2,1)} concatenate(bf16[8,2592]{0,1:T(8,128)(2,1)} %copy.25, bf16[8,2592]{0,1:T(8,128)(2,1)} %copy.26, bf16[8,2592]{0,1:T(8,128)(2,1)} %copy.27, bf16[8,2592]{0,1:T(8,128)(2,1)} %copy.28, bf16[32,2592]{0,1:T(8,128)(2,1)} %copy.29, bf16[16,2592]{0,1:T(8,128)(2,1)} %copy.30, bf16[16,2592]{0,1:T(8,128)(2,1)} %copy.31, bf16[32,2592]{0,1:T(8,128)(2,1)} %copy.32), dimensions={0} | concatenate | bytes 1327104 | tf_op jit(solution)/shard_map/concatenate | solution.py:339
  152.7 2.8 %collective-permute-start.27 = (bf16[2592,128]{1,0:T(8,128)(2,1)}, bf16[2592,128]{1,0:T(8,128)(2,1)S(1)}, u32[]{:S(2)}, u32[]{:S(2)}) collective-permute-start(bf16[2592,128]{1,0:T(8,128)(2,1)} %bitcast.5), channel_id=1, source_target_pairs={{16,0},{18,2},{20,4},{22,6},{24,8},{26,10},{28,12},{30,14},{32,16}... | collective-permute-start | bytes 1990664 | tf_op jit(solution)/shard_map/ppermute | solution.py:320
  156.5 1.9 collective-permute-start.18
  160.1 8.9 %collective-permute-done.29.refs_14_ = bf16[2592,128]{1,0:T(8,128)(2,1)S(1)} collective-permute-done((bf16[2592,128]{1,0:T(8,128)(2,1)}, bf16[2592,128]{1,0:T(8,128)(2,1)S(1)}, u32[]{:S(2)}, u32[]{:S(2)}) %collective-permute-start.29) | collective-permute-done | bytes 663584 | tf_op jit(solution)/shard_map/ppermute | solution.py:320
  169.1 3.6 %collective-permute-start.16 = (bf16[1296,128]{1,0:T(8,128)(2,1)}, bf16[1296,128]{1,0:T(8,128)(2,1)}, u32[]{:S(2)}, u32[]{:S(2)}) collective-permute-start(bf16[1296,128]{1,0:T(8,128)(2,1)} %slice.50), channel_id=1, source_target_pairs={{64,0},{66,2},{68,4},{70,6},{72,8},{74,10},{76,12},{78,14},{80,16}... | collective-permute-start | bytes 995336 | tf_op jit(solution)/shard_map/ppermute | solution.py:320
  175.8 2.7 %collective-permute-start.28 = (bf16[1296,128]{1,0:T(8,128)(2,1)}, bf16[1296,128]{1,0:T(8,128)(2,1)}, u32[]{:S(2)}, u32[]{:S(2)}) collective-permute-start(bf16[1296,128]{1,0:T(8,128)(2,1)} %slice.54), channel_id=1, source_target_pairs={{16,0},{18,2},{20,4},{22,6},{24,8},{26,10},{28,12},{30,14},{32,16}... | collective-permute-start | bytes 995336 | tf_op jit(solution)/shard_map/ppermute | solution.py:320
  178.6 3.9 %collective-permute-done.30.refs_13_ = bf16[1296,128]{1,0:T(8,128)(2,1)} collective-permute-done((bf16[1296,128]{1,0:T(8,128)(2,1)}, bf16[1296,128]{1,0:T(8,128)(2,1)}, u32[]{:S(2)}, u32[]{:S(2)}) %collective-permute-start.30) | collective-permute-done | bytes 331808 | tf_op jit(solution)/shard_map/ppermute | solution.py:320
  186.3 51.9 %solve_columns.1 = bf16[40,36,8,128]{3,2,1,0:T(8,128)(2,1)} custom-call(s32[8,128]{1,0:T(8,128)S(1)} %add_select_fusion.10.refs_0_, bf16[18,8,40,128]{3,2,1,0:T(8,128)(2,1)} %copy-done.2, bf16[18,8,40,128]{3,2,1,0:T(8,128)(2,1)} %copy-done.1, bf16[18,8,40,128]{3,2,1,0:T(8,128)(2,1)} %collective-permute-done.6.refs_3_, ...), custom_call_target="tpu_custom_call" | custom-call | flops 212336640 | bytes 12582912 | tf_op jit(solution)/shard_map/solve_columns/pallas_call | solution.py:285
  (133 shorter events, 52.4 us)
Async XLA Ops:
  2.4 53.2 %collective-permute-start.21 = (bf16[8,2592]{1,0:T(8,128)(2,1)}, bf16[8,2592]{1,0:T(8,128)(2,1)S(1)}, u32[]{:S(2)}, u32[]{:S(2)}) collective-permute-start(bf16[8,2592]{1,0:T(8,128)(2,1)} %copy.10), channel_id=1, source_target_pairs={{12,0},{14,2},{0,4},{2,6},{4,8},{6,10},{8,12},{10,14},{28,16},{30,... | collective-permute-start | bytes 124424 | tf_op jit(solution)/shard_map/ppermute | solution.py:320
  6.2 45.9 %collective-permute-start.20 = (bf16[8,2592]{1,0:T(8,128)(2,1)}, bf16[8,2592]{1,0:T(8,128)(2,1)S(1)}, u32[]{:S(2)}, u32[]{:S(2)}) collective-permute-start(bf16[8,2592]{1,0:T(8,128)(2,1)} %copy.10), channel_id=1, source_target_pairs={{10,0},{12,2},{14,4},{0,6},{2,8},{4,10},{6,12},{8,14},{26,16},{28,... | collective-permute-start | bytes 124424 | tf_op jit(solution)/shard_map/ppermute | solution.py:320
  10.9 25.8 %collective-permute-start.10 = (bf16[8,2592]{1,0:T(8,128)(2,1)}, bf16[8,2592]{1,0:T(8,128)(2,1)S(1)}, u32[]{:S(2)}, u32[]{:S(2)}) collective-permute-start(bf16[8,2592]{1,0:T(8,128)(2,1)} %copy.10), channel_id=1, source_target_pairs={{6,0},{8,2},{10,4},{12,6},{14,8},{0,10},{2,12},{4,14},{22,16},{24,... | collective-permute-start | bytes 124424 | tf_op jit(solution)/shard_map/ppermute | solution.py:320
  10.9 28.3 %collective-permute-start.9 = (bf16[8,2592]{1,0:T(8,128)(2,1)}, bf16[8,2592]{1,0:T(8,128)(2,1)S(1)}, u32[]{:S(2)}, u32[]{:S(2)}) collective-permute-start(bf16[8,2592]{1,0:T(8,128)(2,1)} %copy.10), channel_id=1, source_target_pairs={{4,0},{6,2},{8,4},{10,6},{12,8},{14,10},{0,12},{2,14},{20,16},{22,... | collective-permute-start | bytes 124424 | tf_op jit(solution)/shard_map/ppermute | solution.py:320
  13.7 27.0 %collective-permute-start.8 = (bf16[8,2592]{1,0:T(8,128)(2,1)}, bf16[8,2592]{1,0:T(8,128)(2,1)S(1)}, u32[]{:S(2)}, u32[]{:S(2)}) collective-permute-start(bf16[8,2592]{1,0:T(8,128)(2,1)} %copy.10), channel_id=1, source_target_pairs={{2,0},{4,2},{6,4},{8,6},{10,8},{12,10},{14,12},{0,14},{18,16},{20,... | collective-permute-start | bytes 124424 | tf_op jit(solution)/shard_map/ppermute | solution.py:320
  36.7 7.1 %collective-permute-start.19 = (bf16[8,2592]{1,0:T(8,128)(2,1)}, bf16[8,2592]{1,0:T(8,128)(2,1)S(1)}, u32[]{:S(2)}, u32[]{:S(2)}) collective-permute-start(bf16[8,2592]{1,0:T(8,128)(2,1)} %copy.10), channel_id=1, source_target_pairs={{8,0},{10,2},{12,4},{14,6},{0,8},{2,10},{4,12},{6,14},{24,16},{26,... | collective-permute-start | bytes 124424 | tf_op jit(solution)/shard_map/ppermute | solution.py:320
  39.2 16.3 %collective-permute-start.2 = (bf16[36,2,128]{2,1,0:T(2,128)(2,1)S(1)}, bf16[36,2,128]{2,1,0:T(2,128)(2,1)S(1)}, u32[]{:S(2)}, u32[]{:S(2)}) collective-permute-start(bf16[36,2,128]{2,1,0:T(2,128)(2,1)S(1)} %pad_maximum_fusion.2), channel_id=1, source_target_pairs={{0,2},{2,4},{4,6},{6,8},{8,10},{10,12},{12,14},{14,16},{16,18},{18... | collective-permute-start | bytes 55304 | tf_op jit(solution)/shard_map/ppermute | solution.py:372
  42.1 6.0 %collective-permute-start.13 = (bf16[32,2592]{1,0:T(8,128)(2,1)S(1)}, bf16[32,2592]{1,0:T(8,128)(2,1)S(1)}, u32[]{:S(2)}, u32[]{:S(2)}) collective-permute-start(bf16[32,2592]{1,0:T(8,128)(2,1)S(1)} %pad_maximum_fusion), channel_id=1, source_target_pairs={{48,0},{50,2},{52,4},{54,6},{56,8},{58,10},{60,12},{62,14},{0,16},... | collective-permute-start | bytes 497672 | tf_op jit(solution)/shard_map/ppermute | solution.py:320
  43.8 39.5 %copy-start.22 = (bf16[8,2592]{1,0:T(8,128)(2,1)}, bf16[8,2592]{1,0:T(8,128)(2,1)S(1)}, u32[]{:S(2)}) copy-start(bf16[8,2592]{1,0:T(8,128)(2,1)S(1)} %collective-permute-done.19) | copy-start | bytes 124420
  43.8 8.3 %collective-permute-start.11 = (bf16[32,2592]{1,0:T(8,128)(2,1)S(1)}, bf16[32,2592]{1,0:T(8,128)(2,1)S(1)}, u32[]{:S(2)}, u32[]{:S(2)}) collective-permute-start(bf16[32,2592]{1,0:T(8,128)(2,1)S(1)} %pad_maximum_fusion), channel_id=1, source_target_pairs={{16,0},{18,2},{20,4},{22,6},{24,8},{26,10},{28,12},{30,14},{32,16}... | collective-permute-start | bytes 497672 | tf_op jit(solution)/shard_map/ppermute | solution.py:320
  48.1 7.4 %collective-permute-start.3 = (bf16[36,2,128]{2,1,0:T(2,128)(2,1)S(1)}, bf16[36,2,128]{2,1,0:T(2,128)(2,1)S(1)}, u32[]{:S(2)}, u32[]{:S(2)}) collective-permute-start(bf16[36,2,128]{2,1,0:T(2,128)(2,1)S(1)} %pad_maximum_fusion.3), channel_id=1, source_target_pairs={{2,0},{4,2},{6,4},{8,6},{10,8},{12,10},{14,12},{16,14},{18,16},{20... | collective-permute-start | bytes 55304 | tf_op jit(solution)/shard_map/ppermute | solution.py:373
  52.0 10.5 %collective-permute-start.14 = (bf16[16,2592]{1,0:T(8,128)(2,1)S(1)}, bf16[16,2592]{1,0:T(8,128)(2,1)S(1)}, u32[]{:S(2)}, u32[]{:S(2)}) collective-permute-start(bf16[16,2592]{1,0:T(8,128)(2,1)S(1)} %slice.49), channel_id=1, source_target_pairs={{48,0},{50,2},{52,4},{54,6},{56,8},{58,10},{60,12},{62,14},{0,16},... | collective-permute-start | bytes 248840 | tf_op jit(solution)/shard_map/ppermute | solution.py:320
  52.2 11.0 %collective-permute-start.12 = (bf16[16,2592]{1,0:T(8,128)(2,1)S(1)}, bf16[16,2592]{1,0:T(8,128)(2,1)S(1)}, u32[]{:S(2)}, u32[]{:S(2)}) collective-permute-start(bf16[16,2592]{1,0:T(8,128)(2,1)S(1)} %slice.48), channel_id=1, source_target_pairs={{16,0},{18,2},{20,4},{22,6},{24,8},{26,10},{28,12},{30,14},{32,16}... | collective-permute-start | bytes 248840 | tf_op jit(solution)/shard_map/ppermute | solution.py:320
  55.5 33.7 %collective-permute-start.22 = (bf16[8,2592]{1,0:T(8,128)(2,1)}, bf16[8,2592]{1,0:T(8,128)(2,1)S(1)}, u32[]{:S(2)}, u32[]{:S(2)}) collective-permute-start(bf16[8,2592]{1,0:T(8,128)(2,1)} %copy.10), channel_id=1, source_target_pairs={{14,0},{0,2},{2,4},{4,6},{6,8},{8,10},{10,12},{12,14},{30,16},{16,... | collective-permute-start | bytes 124424 | tf_op jit(solution)/shard_map/ppermute | solution.py:320
  55.5 34.4 %collective-permute-start.4 = (bf16[18,2,40,128]{3,2,1,0:T(8,128)(2,1)S(1)}, bf16[18,2,40,128]{3,2,1,0:T(8,128)(2,1)S(1)}, u32[]{:S(2)}, u32[]{:S(2)}) collective-permute-start(bf16[18,2,40,128]{3,2,1,0:T(8,128)(2,1)S(1)} %get-tuple-element.15), channel_id=1, source_target_pairs={{0,2},{2,4},{4,6},{6,8},{8,10},{10,12},{12,14},{14,16},{16,18},{18... | collective-permute-start | bytes 1105928 | tf_op jit(solution)/shard_map/ppermute | solution.py:382
  55.6 37.0 %collective-permute-start.5 = (bf16[18,2,40,128]{3,2,1,0:T(8,128)(2,1)S(1)}, bf16[18,2,40,128]{3,2,1,0:T(8,128)(2,1)S(1)}, u32[]{:S(2)}, u32[]{:S(2)}) collective-permute-start(bf16[18,2,40,128]{3,2,1,0:T(8,128)(2,1)S(1)} %get-tuple-element.16), channel_id=1, source_target_pairs={{2,0},{4,2},{6,4},{8,6},{10,8},{12,10},{14,12},{16,14},{18,16},{20... | collective-permute-start | bytes 1105928 | tf_op jit(solution)/shard_map/ppermute | solution.py:383
  63.1 43.7 %collective-permute-start = (bf16[18,2,40,128]{3,2,1,0:T(8,128)(2,1)}, bf16[18,2,40,128]{3,2,1,0:T(8,128)(2,1)S(1)}, u32[]{:S(2)}, u32[]{:S(2)}) collective-permute-start(bf16[18,2,40,128]{3,2,1,0:T(8,128)(2,1)} %get-tuple-element.12), channel_id=1, source_target_pairs={{0,2},{2,4},{4,6},{6,8},{8,10},{10,12},{12,14},{14,16},{16,18},{18... | collective-permute-start | bytes 1105928 | tf_op jit(solution)/shard_map/ppermute | solution.py:382
  63.8 43.9 %collective-permute-start.1 = (bf16[18,2,40,128]{3,2,1,0:T(8,128)(2,1)}, bf16[18,2,40,128]{3,2,1,0:T(8,128)(2,1)S(1)}, u32[]{:S(2)}, u32[]{:S(2)}) collective-permute-start(bf16[18,2,40,128]{3,2,1,0:T(8,128)(2,1)} %get-tuple-element.13), channel_id=1, source_target_pairs={{2,0},{4,2},{6,4},{8,6},{10,8},{12,10},{14,12},{16,14},{18,16},{20... | collective-permute-start | bytes 1105928 | tf_op jit(solution)/shard_map/ppermute | solution.py:383
  89.2 63.6 %collective-permute-start.17 = (bf16[2592,128]{1,0:T(8,128)(2,1)}, bf16[2592,128]{1,0:T(8,128)(2,1)}, u32[]{:S(2)}, u32[]{:S(2)}) collective-permute-start(bf16[2592,128]{1,0:T(8,128)(2,1)} %bitcast.2.refs_5_), channel_id=1, source_target_pairs={{192,0},{194,2},{196,4},{198,6},{200,8},{202,10},{204,12},{206,14}... | collective-permute-start | bytes 1990664 | tf_op jit(solution)/shard_map/ppermute | solution.py:320
  89.9 27.1 %collective-permute-start.23 = (bf16[32,2592]{1,0:T(8,128)(2,1)}, bf16[32,2592]{1,0:T(8,128)(2,1)S(1)}, u32[]{:S(2)}, u32[]{:S(2)}) collective-permute-start(bf16[32,2592]{1,0:T(8,128)(2,1)} %constant_dynamic-update-slice_fusion), channel_id=1, source_target_pairs={{64,0},{66,2},{68,4},{70,6},{72,8},{74,10},{76,12},{78,14},{80,16}... | collective-permute-start | bytes 497672 | tf_op jit(solution)/shard_map/ppermute | solution.py:320
  100.9 82.2 %collective-permute-start.7 = (bf16[18,8,40,128]{3,2,1,0:T(8,128)(2,1)S(1)}, bf16[18,8,40,128]{3,2,1,0:T(8,128)(2,1)}, u32[]{:S(2)}, u32[]{:S(2)}) collective-permute-start(bf16[18,8,40,128]{3,2,1,0:T(8,128)(2,1)S(1)} %transport_second.3.refs_2_), channel_id=1, source_target_pairs={{0,1},{1,0},{2,3},{3,2},{4,5},{5,4},{6,7},{7,6},{8,9},{9,8},{10,11... | collective-permute-start | bytes 4423688 | tf_op jit(solution)/shard_map/ppermute | solution.py:388
  116.8 66.2 %collective-permute-start.6 = (bf16[18,8,40,128]{3,2,1,0:T(8,128)(2,1)S(1)}, bf16[18,8,40,128]{3,2,1,0:T(8,128)(2,1)}, u32[]{:S(2)}, u32[]{:S(2)}) collective-permute-start(bf16[18,8,40,128]{3,2,1,0:T(8,128)(2,1)S(1)} %transport_second.2.refs_1_), channel_id=1, source_target_pairs={{0,1},{1,0},{2,3},{3,2},{4,5},{5,4},{6,7},{7,6},{8,9},{9,8},{10,11... | collective-permute-start | bytes 4423688 | tf_op jit(solution)/shard_map/ppermute | solution.py:388
  117.0 7.0 %collective-permute-start.25 = (bf16[32,2592]{1,0:T(8,128)(2,1)}, bf16[32,2592]{1,0:T(8,128)(2,1)S(1)}, u32[]{:S(2)}, u32[]{:S(2)}) collective-permute-start(bf16[32,2592]{1,0:T(8,128)(2,1)} %constant_dynamic-update-slice_fusion), channel_id=1, source_target_pairs={{192,0},{194,2},{196,4},{198,6},{200,8},{202,10},{204,12},{206,14}... | collective-permute-start | bytes 497672 | tf_op jit(solution)/shard_map/ppermute | solution.py:320
  117.0 39.5 %collective-permute-start.15 = (bf16[2592,128]{1,0:T(8,128)(2,1)}, bf16[2592,128]{1,0:T(8,128)(2,1)}, u32[]{:S(2)}, u32[]{:S(2)}) collective-permute-start(bf16[2592,128]{1,0:T(8,128)(2,1)} %bitcast.2.refs_5_), channel_id=1, source_target_pairs={{64,0},{66,2},{68,4},{70,6},{72,8},{74,10},{76,12},{78,14},{80,16}... | collective-permute-start | bytes 1990664 | tf_op jit(solution)/shard_map/ppermute | solution.py:320
  124.0 11.3 %collective-permute-start.24 = (bf16[16,2592]{1,0:T(8,128)(2,1)S(1)}, bf16[16,2592]{1,0:T(8,128)(2,1)S(1)}, u32[]{:S(2)}, u32[]{:S(2)}) collective-permute-start(bf16[16,2592]{1,0:T(8,128)(2,1)S(1)} %slice.52), channel_id=1, source_target_pairs={{64,0},{66,2},{68,4},{70,6},{72,8},{74,10},{76,12},{78,14},{80,16}... | collective-permute-start | bytes 248840 | tf_op jit(solution)/shard_map/ppermute | solution.py:320
  135.4 9.4 %collective-permute-start.26 = (bf16[16,2592]{1,0:T(8,128)(2,1)}, bf16[16,2592]{1,0:T(8,128)(2,1)}, u32[]{:S(2)}, u32[]{:S(2)}) collective-permute-start(bf16[16,2592]{1,0:T(8,128)(2,1)} %slice.53), channel_id=1, source_target_pairs={{192,0},{194,2},{196,4},{198,6},{200,8},{202,10},{204,12},{206,14}... | collective-permute-start | bytes 248840 | tf_op jit(solution)/shard_map/ppermute | solution.py:320
  152.7 16.3 %collective-permute-start.29 = (bf16[2592,128]{1,0:T(8,128)(2,1)}, bf16[2592,128]{1,0:T(8,128)(2,1)S(1)}, u32[]{:S(2)}, u32[]{:S(2)}) collective-permute-start(bf16[2592,128]{1,0:T(8,128)(2,1)} %bitcast.4), channel_id=1, source_target_pairs={{48,0},{50,2},{52,4},{54,6},{56,8},{58,10},{60,12},{62,14},{0,16},... | collective-permute-start | bytes 1990664 | tf_op jit(solution)/shard_map/ppermute | solution.py:320
  152.7 21.5 %collective-permute-start.27 = (bf16[2592,128]{1,0:T(8,128)(2,1)}, bf16[2592,128]{1,0:T(8,128)(2,1)S(1)}, u32[]{:S(2)}, u32[]{:S(2)}) collective-permute-start(bf16[2592,128]{1,0:T(8,128)(2,1)} %bitcast.5), channel_id=1, source_target_pairs={{16,0},{18,2},{20,4},{22,6},{24,8},{26,10},{28,12},{30,14},{32,16}... | collective-permute-start | bytes 1990664 | tf_op jit(solution)/shard_map/ppermute | solution.py:320
  156.5 19.3 %collective-permute-start.18 = (bf16[1296,128]{1,0:T(8,128)(2,1)S(1)}, bf16[1296,128]{1,0:T(8,128)(2,1)S(1)}, u32[]{:S(2)}, u32[]{:S(2)}) collective-permute-start(bf16[1296,128]{1,0:T(8,128)(2,1)S(1)} %slice.51), channel_id=1, source_target_pairs={{192,0},{194,2},{196,4},{198,6},{200,8},{202,10},{204,12},{206,14}... | collective-permute-start | bytes 995336 | tf_op jit(solution)/shard_map/ppermute | solution.py:320
  169.1 9.5 %collective-permute-start.16 = (bf16[1296,128]{1,0:T(8,128)(2,1)}, bf16[1296,128]{1,0:T(8,128)(2,1)}, u32[]{:S(2)}, u32[]{:S(2)}) collective-permute-start(bf16[1296,128]{1,0:T(8,128)(2,1)} %slice.50), channel_id=1, source_target_pairs={{64,0},{66,2},{68,4},{70,6},{72,8},{74,10},{76,12},{78,14},{80,16}... | collective-permute-start | bytes 995336 | tf_op jit(solution)/shard_map/ppermute | solution.py:320
  174.2 8.2 %collective-permute-start.30 = (bf16[1296,128]{1,0:T(8,128)(2,1)}, bf16[1296,128]{1,0:T(8,128)(2,1)}, u32[]{:S(2)}, u32[]{:S(2)}) collective-permute-start(bf16[1296,128]{1,0:T(8,128)(2,1)} %slice.55), channel_id=1, source_target_pairs={{48,0},{50,2},{52,4},{54,6},{56,8},{58,10},{60,12},{62,14},{0,16},... | collective-permute-start | bytes 995336 | tf_op jit(solution)/shard_map/ppermute | solution.py:320
  175.8 7.2 %collective-permute-start.28 = (bf16[1296,128]{1,0:T(8,128)(2,1)}, bf16[1296,128]{1,0:T(8,128)(2,1)}, u32[]{:S(2)}, u32[]{:S(2)}) collective-permute-start(bf16[1296,128]{1,0:T(8,128)(2,1)} %slice.54), channel_id=1, source_target_pairs={{16,0},{18,2},{20,4},{22,6},{24,8},{26,10},{28,12},{30,14},{32,16}... | collective-permute-start | bytes 995336 | tf_op jit(solution)/shard_map/ppermute | solution.py:320
  (29 other events, 186.1 us)

commit v2 on v1

v2 whole, which is shorter than its diff:
```python
import functools

import jax
import jax.numpy as jnp
import numpy as np
from jax import lax
from jax.experimental import pallas as pl
from jax.experimental.pallas import tpu as pltpu
from jax.sharding import PartitionSpec as P

NP = 4
TIME_STEP = 0.08
NY_CHIPS, NX_CHIPS, NZ_CHIPS = 4, 4, 8
ELEM = ("y", "x", "z")
CHUNKS = 2
LANES = 128
TRIPLES = ((0, 1, 2), (3, 4, 5), (6, 7))
HEIGHT = 48
F32, BF16 = jnp.float32, jnp.bfloat16


def derivative_table():
    nodes = np.array([-1.0, -1.0 / np.sqrt(5.0), 1.0 / np.sqrt(5.0), 1.0])
    table = np.zeros((NP, NP))
    for i in range(NP):
        for k in range(NP):
            if i == k:
                table[i, k] = sum(1.0 / (nodes[i] - nodes[m]) for m in range(NP) if m != i)
            else:
                top = np.prod([nodes[i] - nodes[m] for m in range(NP) if m != k and m != i])
                table[i, k] = top / np.prod([nodes[k] - nodes[m] for m in range(NP) if m != k])
    return table


D = derivative_table()
D = [[float(D[i, k]) for k in range(NP)] for i in range(NP)]


def table_y(width):
    full = np.kron(np.eye(width // NP), np.array(D)).T.astype(np.float32)
    hi = full.astype(jnp.bfloat16)
    lo = (full - hi.astype(np.float32)).astype(jnp.bfloat16)
    first = np.concatenate([hi, lo], axis=0)
    zero = np.zeros_like(lo)
    second = np.concatenate(
        [np.concatenate([hi, lo], axis=1), np.concatenate([hi, zero], axis=1)], axis=0
    )
    mean = np.eye(width)
    for y in range(width):
        if y % NP in (0, NP - 1):
            mean[y, y] = mean[y, (y + (1 if y % NP else -1)) % width] = 0.5
    mean = np.concatenate([mean, mean], axis=1).astype(jnp.bfloat16)
    return jnp.asarray(first), jnp.asarray(second), jnp.asarray(mean)


def grad_x(s0, s1, s2, s3):
    m, n = s3 - s0, s2 - s1
    e = (s0 + s3) - (s1 + s2)
    a = 0.5 * (D[3][3] + D[0][3])
    b = 0.5 * (D[0][1] + D[3][1])
    u = a * m - b * n
    v = (0.5 * (D[1][3] + D[2][3])) * m + (0.5 * (D[1][2] + D[2][2])) * n
    w = (0.5 * (D[3][3] - D[0][3])) * e
    z = (0.5 * (D[2][3] - D[1][3])) * e
    return [u - w, v - z, v + z, u + w]


def mean_y(value, last, inner):
    width = value.shape[1]
    ahead = pltpu.roll(value, width - 1, axis=1)
    behind = pltpu.roll(value, 1, axis=1)
    return jnp.where(inner, value, 0.5 * (value + jnp.where(last, ahead, behind)))


def node_masks(shape):
    node = lax.broadcasted_iota(jnp.int32, shape, 1) % NP
    return node == NP - 1, (node == 1) | (node == 2)


def first_kernel(levels, t_ref, wx_ref, wy_ref, d_ref, st_ref, dn_ref, up_ref, scr):
    groups, width_x, width_y = t_ref.shape[0], t_ref.shape[2], t_ref.shape[3]
    last, inner = node_masks((groups, width_y))

    @pl.loop(0, levels, unroll=3)
    def _(l):
        scr[...] = t_ref[:, l].astype(F32).reshape(groups * width_x, width_y)
        s = [scr[pl.ds(x, groups, stride=width_x), :] for x in range(width_x)]
        wx = wx_ref[l].astype(F32) * TIME_STEP
        wy = wy_ref[l].astype(F32) * TIME_STEP
        flat = jnp.concatenate(s, axis=0).astype(BF16)
        gy = jnp.dot(
            jnp.concatenate([flat, flat], axis=1), d_ref[...], preferred_element_type=F32
        )
        gx = grad_x(*s[:4]) + grad_x(*s[4:])
        adv = [
            s[x]
            - (wx[x : x + 1] * gx[x] + wy[x : x + 1] * gy[x * groups : (x + 1) * groups])
            for x in range(width_x)
        ]
        middle = mean_y(0.5 * (adv[3] + adv[4]), last, inner)
        st = [adv[0], None, None, middle, middle, None, None, adv[7]]
        for x in (1, 2, 5, 6):
            st[x] = mean_y(adv[x], last, inner)
        for x in range(width_x):
            st_ref[l, x] = st[x]
        part = D[0][1] * st[1] + D[0][2] * st[2] + D[0][3] * st[3]
        dn_ref[l, 0] = adv[0].astype(BF16)
        dn_ref[l, 1] = (-wx[0:1] * part).astype(BF16)
        part = D[3][0] * st[4] + D[3][1] * st[5] + D[3][2] * st[6]
        up_ref[l, 0] = adv[7].astype(BF16)
        up_ref[l, 1] = (-wx[7:8] * part).astype(BF16)


def second_kernel(
    levels, st_ref, left_ref, right_ref, wx_ref, wy_ref, wl_ref, wr_ref, d_ref, m_ref, out_ref
):
    width_x, groups, width_y = st_ref.shape[1:]
    last, inner = node_masks((groups, width_y))

    @pl.loop(0, levels, unroll=3)
    def _(l):
        s = [None] + [st_ref[l, x] for x in range(1, 7)] + [None]
        s[0] = mean_y(0.5 * (st_ref[l, 0] + left_ref[l, 0].astype(F32)), last, inner)
        s[7] = mean_y(0.5 * (st_ref[l, 7] + right_ref[l, 0].astype(F32)), last, inner)
        wx = wx_ref[l].astype(F32) * TIME_STEP
        wy = wy_ref[l].astype(F32) * TIME_STEP
        wl = wl_ref[l].astype(F32) * TIME_STEP
        wr = wr_ref[l].astype(F32) * TIME_STEP
        flat = jnp.concatenate(s, axis=0)
        hi = flat.astype(BF16)
        lo = (flat - hi.astype(F32)).astype(BF16)
        both = jnp.dot(
            jnp.concatenate([hi, lo], axis=1), d_ref[...], preferred_element_type=F32
        )
        gy = both[:, :width_y] + both[:, width_y:]
        gys = [gy[x * groups : (x + 1) * groups] for x in range(width_x)]
        gx = grad_x(*s[:4]) + grad_x(*s[4:])
        adv = [
            s[x] - (wx[x : x + 1] * gx[x] + wy[x : x + 1] * gys[x]) for x in range(width_x)
        ]
        before = (
            s[0]
            - ((wl[0:1] * D[3][3]) * s[0] + wl[1:2] * gys[0])
            + left_ref[l, 1].astype(F32)
        )
        after = (
            s[7]
            - ((wr[0:1] * D[0][0]) * s[7] + wr[1:2] * gys[7])
            + right_ref[l, 1].astype(F32)
        )
        middle = 0.5 * (adv[3] + adv[4])
        adv[0] = 0.5 * (before + adv[0])
        adv[7] = 0.5 * (adv[7] + after)
        adv[3] = adv[4] = middle
        for g, triple in enumerate(TRIPLES):
            rest = jnp.zeros((LANES - len(triple) * groups, width_y), F32)
            flat = jnp.concatenate([adv[x] for x in triple] + [rest], axis=0)
            hi = flat.astype(BF16)
            lo = (flat - hi.astype(F32)).astype(BF16)
            out_ref[l, g] = lax.dot_general(
                m_ref[...],
                jnp.concatenate([hi, lo], axis=1),
                (((1,), (1,)), ((), ())),
                preferred_element_type=F32,
            ).astype(BF16)


def first_part(tracers, wind_x, wind_y, table, start, count):
    groups, _, width_x, width_y = tracers.shape
    step = 3
    skip = start // step
    spec_w = pl.BlockSpec((step, width_x, width_y), lambda i: (i + skip, 0, 0))
    spec_m = pl.BlockSpec((step, 2, groups, width_y), lambda i: (i, 0, 0, 0))
    return pl.pallas_call(
        lambda *refs: first_kernel(step, *refs),
        grid=(count // step,),
        in_specs=[
            pl.BlockSpec((groups, step, width_x, width_y), lambda i: (0, i + skip, 0, 0)),
            spec_w,
            spec_w,
            pl.BlockSpec(table.shape, lambda i: (0, 0)),
        ],
        out_specs=[
            pl.BlockSpec((step, width_x, groups, width_y), lambda i: (i, 0, 0, 0)),
            spec_m,
            spec_m,
        ],
        out_shape=[
            jax.ShapeDtypeStruct((count, width_x, groups, width_y), F32),
            jax.ShapeDtypeStruct((count, 2, groups, width_y), BF16),
            jax.ShapeDtypeStruct((count, 2, groups, width_y), BF16),
        ],
        scratch_shapes=[pltpu.VMEM((groups * width_x, width_y), F32)],
        compiler_params=pltpu.CompilerParams(vmem_limit_bytes=24 << 20),
        cost_estimate=pl.CostEstimate(
            flops=40 * count * width_x * groups * width_y,
            bytes_accessed=8 * count * width_x * groups * width_y,
            transcendentals=0,
        ),
        name="transport_first",
    )(tracers, wind_x, wind_y, table)


def second_part(
    state, left, right, wind_x, wind_y, wind_l, wind_r, table, mean, start
):
    count, width_x, groups, width_y = state.shape
    step = 3
    skip = start // step
    spec_s = pl.BlockSpec((step, width_x, groups, width_y), lambda i: (i, 0, 0, 0))
    spec_m = pl.BlockSpec((step, 2, groups, width_y), lambda i: (i, 0, 0, 0))
    spec_w = pl.BlockSpec((step, width_x, width_y), lambda i: (i + skip, 0, 0))
    spec_n = pl.BlockSpec((step, 2, width_y), lambda i: (i + skip, 0, 0))
    return pl.pallas_call(
        lambda *refs: second_kernel(step, *refs),
        grid=(count // step,),
        in_specs=[
            spec_s, spec_m, spec_m, spec_w, spec_w, spec_n, spec_n,
            pl.BlockSpec(table.shape, lambda i: (0, 0)),
            pl.BlockSpec(mean.shape, lambda i: (0, 0)),
        ],
        out_specs=pl.BlockSpec(
            (step, len(TRIPLES), width_y, LANES), lambda i: (i, 0, 0, 0)
        ),
        out_shape=jax.ShapeDtypeStruct((count, len(TRIPLES), width_y, LANES), BF16),
        compiler_params=pltpu.CompilerParams(vmem_limit_bytes=24 << 20),
        cost_estimate=pl.CostEstimate(
            flops=40 * count * width_x * groups * width_y,
            bytes_accessed=8 * count * width_x * groups * width_y,
            transcendentals=0,
        ),
        name="transport_second",
    )(state, left, right, wind_x, wind_y, wind_l, wind_r, table, mean)


def solve_kernel(n_fields, n_pieces, pos_ref, *refs):
    fields = refs[:n_fields]
    pieces = refs[n_fields : n_fields + n_pieces]
    out_ref = refs[n_fields + n_pieces]
    matrices, value, result, final = refs[n_fields + n_pieces + 1 :]
    groups, rows, width_x, width_y = out_ref.shape
    levels = value.shape[0] // width_y
    per_block = pieces[0].shape[2] // levels

    base = 0
    for piece in pieces:
        count = piece.shape[0]

        @pl.loop(0, count)
        def _(k, piece=piece, base=base):
            for j in range(per_block):
                tile, shift = divmod(j * levels, LANES)
                part = piece[k, :, tile * LANES : (tile + 1) * LANES].astype(F32)
                if shift:
                    part = pltpu.roll(part, LANES - shift, axis=1)
                if shift + levels > LANES:
                    after = piece[k, :, (tile + 1) * LANES : (tile + 2) * LANES].astype(F32)
                    after = pltpu.roll(after, LANES - shift, axis=1)
                    lane = lax.broadcasted_iota(jnp.int32, after.shape, 1)
                    part = jnp.where(lane < LANES - shift, part, after)
                matrices[(base + k) * per_block + j, : part.shape[0]] = part.astype(BF16)

        base += count

    lane = lax.broadcasted_iota(jnp.int32, (rows, LANES), 1)
    eye = (
        lax.broadcasted_iota(jnp.int32, (LANES, LANES), 0)
        == lax.broadcasted_iota(jnp.int32, (LANES, LANES), 1)
    ).astype(F32).astype(BF16)
    for g, triple in enumerate(TRIPLES):
        level = 0
        for field in fields:
            for l in range(field.shape[0]):
                value[pl.ds(level, width_y, stride=levels), :] = field[l, g].astype(F32)
                level += 1

        @pl.loop(0, width_y, unroll=16)
        def _(y, triple=triple):
            start = pl.multiple_of(y * levels, 8)
            columns = value[pl.ds(start, levels), :]
            columns = jnp.concatenate(
                [columns, jnp.zeros((LANES - levels, LANES), F32)], axis=0
            ).astype(BF16)
            chosen = jnp.concatenate([matrices[pos_ref[x, y]] for x in triple], axis=0)
            product = jnp.dot(chosen, columns, preferred_element_type=F32)
            picked = product[(len(triple) - 1) * HEIGHT :][:rows]
            for i in range(len(triple) - 2, -1, -1):
                picked = jnp.where(
                    lane < (i + 1) * groups, product[i * HEIGHT : i * HEIGHT + rows], picked
                )
            result[pl.ds(y, rows, stride=width_y), :] = picked

        @pl.loop(0, rows, unroll=12)
        def _(a, triple=triple):
            start = pl.multiple_of(a * width_y, width_y)
            solved = result[pl.ds(start, width_y), :].astype(BF16)
            turned = lax.dot_general(
                eye, solved, (((1,), (1,)), ((), ())), preferred_element_type=F32
            )
            for i, x in enumerate(triple):
                final[a, pl.ds(x, groups, stride=width_x), :] = turned[
                    i * groups : (i + 1) * groups
                ]

    @pl.loop(0, rows, unroll=4)
    def _(a):
        out_ref[:, a] = final[a].reshape(groups, width_x, width_y).astype(BF16)


def solve(fields, pieces, position, groups, levels_out, width_x, width_y):
    levels = sum(f.shape[0] for f in fields)
    spans = sum(p.shape[0] * p.shape[2] for p in pieces) // levels
    vmem = pl.BlockSpec(memory_space=pltpu.VMEM)
    return pl.pallas_call(
        functools.partial(solve_kernel, len(fields), len(pieces)),
        in_specs=[pl.BlockSpec(memory_space=pltpu.SMEM)]
        + [vmem] * (len(fields) + len(pieces)),
        out_specs=vmem,
        out_shape=jax.ShapeDtypeStruct((groups, levels_out, width_x, width_y), BF16),
        scratch_shapes=[
            pltpu.VMEM((spans, HEIGHT, LANES), BF16),
            pltpu.VMEM((width_y * levels, LANES), F32),
            pltpu.VMEM((levels_out * width_y, LANES), F32),
            pltpu.VMEM((levels_out, groups * width_x, width_y), F32),
        ],
        compiler_params=pltpu.CompilerParams(vmem_limit_bytes=52 << 20),
        cost_estimate=pl.CostEstimate(
            flops=2 * levels_out * levels * groups * width_x * width_y,
            bytes_accessed=12 << 20,
            transcendentals=0,
        ),
        name="solve_columns",
    )(position, *fields, *pieces)


def elem_index(y, x, z):
    return (y % NY_CHIPS * NX_CHIPS + x % NX_CHIPS) * NZ_CHIPS + z % NZ_CHIPS


def fetch(value, dy=0, dx=0, dz=0):
    pairs = [
        (elem_index(y + dy, x + dx, z + dz), elem_index(y, x, z))
        for y in range(NY_CHIPS)
        for x in range(NX_CHIPS)
        for z in range(NZ_CHIPS)
    ]
    return lax.ppermute(value, ELEM, pairs)


def gather_matrices(block):
    near = [block] + [fetch(block, dz=d) for d in range(1, NZ_CHIPS)]
    part = jnp.concatenate(near, axis=1)
    return [lax.all_gather(part, ("y", "x"), axis=0)]


def span_position(span_ids, per_dev):
    owner, local = span_ids // per_dev, span_ids % per_dev
    dz = (owner % NZ_CHIPS - lax.axis_index("z")) % NZ_CHIPS
    return (owner // NZ_CHIPS * NZ_CHIPS + dz) * per_dev + local


def body(tracers, wind_x, wind_y, span_of, inverses):
    groups, half_levels, width_x, width_y = tracers.shape
    per_dev = inverses.shape[0]
    first_table, second_table, mean = table_y(width_y)
    size = NY_CHIPS * NX_CHIPS * NZ_CHIPS
    up = [(i, (i + 1) % size) for i in range(size)]
    down = [(j, i) for i, j in up]
    lev = lax.axis_index("lev")

    mine = lax.dynamic_slice_in_dim(inverses, lev * half_levels, half_levels, 1)
    own = lax.dynamic_slice_in_dim(mine, lev * half_levels, half_levels, 2)
    other = lax.dynamic_slice_in_dim(mine, (1 - lev) * half_levels, half_levels, 2)
    block = jnp.concatenate([own, other], axis=2).transpose(1, 0, 2)
    block = block.reshape(half_levels, -1)
    block = jnp.pad(block, ((0, -half_levels % 8), (0, 0)))
    pieces = gather_matrices(block)
    position = span_position(span_of[:, 0], per_dev).reshape(width_x, width_y)

    wind_l = lax.ppermute(jnp.stack([wind_x[:, -1], wind_y[:, -1]], 1), ELEM, up)
    wind_r = lax.ppermute(jnp.stack([wind_x[:, 0], wind_y[:, 0]], 1), ELEM, down)

    count = half_levels // CHUNKS
    firsts = [
        first_part(tracers, wind_x, wind_y, first_table, i * count, count)
        for i in range(CHUNKS)
    ]
    own_fields, other_fields = [], []
    for i, (state, to_left, to_right) in enumerate(firsts):
        left = lax.ppermute(to_right, ELEM, up)
        right = lax.ppermute(to_left, ELEM, down)
        field = second_part(
            state, left, right, wind_x, wind_y, wind_l, wind_r, second_table, mean, i * count
        )
        own_fields.append(field)
        other_fields.append(lax.ppermute(field, "lev", [(0, 1), (1, 0)]))
    return solve(
        own_fields + other_fields, pieces, position, groups, half_levels, width_x, width_y
    )


def solution(mesh):
    chips = jax.sharding.Mesh(
        mesh.devices.reshape(NY_CHIPS, NX_CHIPS, NZ_CHIPS, -1), ELEM + ("lev",)
    )
    return jax.shard_map(
        body,
        mesh=chips,
        in_specs=(
            P(None, "lev", ELEM, None),
            P("lev", ELEM, None),
            P("lev", ELEM, None),
            P(ELEM, None),
            P(ELEM, None, None),
        ),
        out_specs=P(None, "lev", ELEM, None),
        check_vma=False,
    )
```

time: 243 us -> 145 us (0.60); the launches traced: 238 us -> 145 us
  local copies, waits for them, and re-layouts: 65.7 us -> 6.66 us
  Pallas kernels: 77 us -> 45.1 us
  starting transfers between devices: 64.1 us -> 35.3 us
  waiting for transfers between devices: 30.1 us -> 43.9 us
  between operations: 0.29 us -> 13.5 us
    ppermute x29 -> x13, starting transfers between devices: 57.9 us -> 31.4 us  [the longest x7 17.3 us: fetch(): return lax.ppermute(value, ELEM, pairs)]
    ppermute x15 -> x0, local copies, waits for them, and re-layouts: 23.3 us -> none  [fetch(): return lax.ppermute(value, 'elem', pairs)]
    all_gather x0 -> x1, waiting for transfers between devices: none -> 23.1 us  [gather_matrices(): return [lax.all_gather(part, ('y', 'x'), axis=0)]]
    pallas_call x1, Pallas kernels: 51.9 us -> 29.6 us  [solve(): pl.pallas_call(functools.partial(solve_kernel, len(fields), len(pieces)),...]
    unnamed x63 -> x16, local copies, waits for them, and re-layouts: 21.6 us -> 4.45 us
    ppermute x29 -> x13, waiting for transfers between devices: 30.1 us -> 17 us  [the longest x1 8.53 us: body(): lax.ppermute(jnp.stack([wind_x[:, -1], wind_y[:, -1]], 1), ELEM, up)]
    concatenate x4 -> x1, local copies, waits for them, and re-layouts: 12.8 us -> 0.92 us  [gather_matrices(): part = jnp.concatenate(near, axis=1)]
    pallas_call x2, Pallas kernels: 12.2 us -> 5.75 us  [first_part(): pl.pallas_call(lambda *refs: first_kernel(step, *refs), grid=(count // st...]
  transfers between devices with their start and end apart: 31 -> 16, of which waited for: 7 -> 6; matrix products, arithmetic and copies ran while one was open for 19% -> 0% of each run, Pallas kernels for 11% -> 11%
where the time goes in v2:
time: 145 us
  Pallas kernels  45.1 us (31%)
  waiting for transfers between devices  43.9 us (30%)
  starting transfers between devices  35.3 us (24%)
  between operations  13.5 us (9%)
  local copies, waits for them, and re-layouts  6.66 us (5%)
    pallas_call x1, Pallas kernels, solve(): pl.pallas_call(functools.partial(solve_kernel, len(fields), len(pieces)),...  29.6 us
    all_gather x1, waiting for transfers between devices, gather_matrices(): return [lax.all_gather(part, ('y', 'x'), axis=0)]  23.1 us
    ppermute x7, starting transfers between devices, fetch(): return lax.ppermute(value, ELEM, pairs)  17.3 us
    ppermute x2, starting transfers between devices, body(): right = lax.ppermute(to_left, ELEM, down)  12.2 us
    pallas_call x2, Pallas kernels, second_part(): pl.pallas_call(lambda *refs: second_kernel(step, *refs), grid=(count // s...  9.72 us
    ppermute x1, waiting for transfers between devices, body(): lax.ppermute(jnp.stack([wind_x[:, -1], wind_y[:, -1]], 1), ELEM, up)  8.53 us
    pallas_call x2, Pallas kernels, first_part(): pl.pallas_call(lambda *refs: first_kernel(step, *refs), grid=(count // st...  5.75 us
    ppermute x7, waiting for transfers between devices, fetch(): return lax.ppermute(value, ELEM, pairs)  5.49 us
  transfers between devices with their start and end apart: 16, of which 6 were waited for; matrix products, arithmetic and copies ran while one was open for 0% of the time, Pallas kernels for 11%

profile of v2, /device:TPU:1, one launch (start us, length us, event | category | flops | bytes accessed | tf_op | source)
XLA Modules:
  0.0 144.7 jit_solution(13865550382403102658)
XLA Ops:
  6.5 1.1 constant_dynamic-slice_fusion.1
  7.6 0.1 maximum_bitcast_fusion
  7.7 0.1 reshape.5
  7.9 2.5 %collective-permute-start.14 = (bf16[40,576]{1,0:T(8,128)(2,1)S(1)}, bf16[40,576]{1,0:T(8,128)(2,1)S(1)}, u32[]{:S(2)}, u32[]{:S(2)}) collective-permute-start(bf16[40,576]{1,0:T(8,128)(2,1)S(1)} %pad.4), channel_id=1, source_target_pairs={{14,0},{0,2},{2,4},{4,6},{6,8},{8,10},{10,12},{12,14},{30,16},{16,... | collective-permute-start | bytes 138248 | tf_op jit(solution)/shard_map/ppermute | solution.py:347
  10.4 3.0 %collective-permute-start.13 = (bf16[40,576]{1,0:T(8,128)(2,1)S(1)}, bf16[40,576]{1,0:T(8,128)(2,1)S(1)}, u32[]{:S(2)}, u32[]{:S(2)}) collective-permute-start(bf16[40,576]{1,0:T(8,128)(2,1)S(1)} %pad.4), channel_id=1, source_target_pairs={{12,0},{14,2},{0,4},{2,6},{4,8},{6,10},{8,12},{10,14},{28,16},{30,... | collective-permute-start | bytes 138248 | tf_op jit(solution)/shard_map/ppermute | solution.py:347
  13.4 3.8 %collective-permute-start.12 = (bf16[40,576]{1,0:T(8,128)(2,1)S(1)}, bf16[40,576]{1,0:T(8,128)(2,1)S(1)}, u32[]{:S(2)}, u32[]{:S(2)}) collective-permute-start(bf16[40,576]{1,0:T(8,128)(2,1)S(1)} %pad.4), channel_id=1, source_target_pairs={{10,0},{12,2},{14,4},{0,6},{2,8},{4,10},{6,12},{8,14},{26,16},{28,... | collective-permute-start | bytes 138248 | tf_op jit(solution)/shard_map/ppermute | solution.py:347
  17.2 0.5 collective-permute-start.11
  17.6 4.5 %collective-permute-start.10 = (bf16[40,576]{1,0:T(8,128)(2,1)S(1)}, bf16[40,576]{1,0:T(8,128)(2,1)S(1)}, u32[]{:S(2)}, u32[]{:S(2)}) collective-permute-start(bf16[40,576]{1,0:T(8,128)(2,1)S(1)} %pad.4), channel_id=1, source_target_pairs={{6,0},{8,2},{10,4},{12,6},{14,8},{0,10},{2,12},{4,14},{22,16},{24,... | collective-permute-start | bytes 138248 | tf_op jit(solution)/shard_map/ppermute | solution.py:347
  22.1 2.4 %collective-permute-start.9 = (bf16[40,576]{1,0:T(8,128)(2,1)S(1)}, bf16[40,576]{1,0:T(8,128)(2,1)S(1)}, u32[]{:S(2)}, u32[]{:S(2)}) collective-permute-start(bf16[40,576]{1,0:T(8,128)(2,1)S(1)} %pad.4), channel_id=1, source_target_pairs={{4,0},{6,2},{8,4},{10,6},{12,8},{14,10},{0,12},{2,14},{20,16},{22,... | collective-permute-start | bytes 138248 | tf_op jit(solution)/shard_map/ppermute | solution.py:347
  24.5 0.7 collective-permute-start.8
  25.2 5.0 %collective-permute-done.9 = bf16[40,576]{1,0:T(8,128)(2,1)S(1)} collective-permute-done((bf16[40,576]{1,0:T(8,128)(2,1)S(1)}, bf16[40,576]{1,0:T(8,128)(2,1)S(1)}, u32[]{:S(2)}, u32[]{:S(2)}) %collective-permute-start.9) | collective-permute-done | bytes 46112 | tf_op jit(solution)/shard_map/ppermute | solution.py:347
  30.3 0.5 collective-permute-done.8
  30.7 0.9 concatenate.7
  31.7 1.8 %copy-done = bf16[40,36,8,128]{3,2,1,0:T(8,128)(2,1)S(1)} copy-done((bf16[40,36,8,128]{3,2,1,0:T(8,128)(2,1)S(1)}, bf16[40,36,8,128]{3,2,1,0:T(8,128)(2,1)}, u32[]{:S(2)}) %copy-start) | copy-done | bytes 2949144
  33.5 0.9 copy-done.2
  34.4 0.9 copy-done.3
  35.3 0.8 copy-done.6
  36.1 2.9 %transport_first.3 = (f32[18,8,40,128]{3,2,1,0:T(8,128)S(1)}, bf16[18,2,40,128]{3,2,1,0:T(8,128)(2,1)S(1)}, bf16[18,2,40,128]{3,2,1,0:T(8,128)(2,1)S(1)}) custom-call(bf16[40,36,8,128]{3,2,1,0:T(8,128)(2,1)S(1)} %copy-done, bf16[36,8,128]{2,1,0:T(8,128)(2,1)S(1)} %copy-done.2, bf16[36,8,128]{2,1,0:T(8,128)(2,1)S(1)} %copy-done.3, bf16[256,128]{1,0:T(8,128)(2,1)S(1)} %copy-done.6), custom_call_target="tpu_custom_call" | custom-call | flops 29491200 | bytes 5898240 | tf_op jit(solution)/shard_map/transport_first/pallas_call | solution.py:174
  39.0 1.7 %collective-permute-start.4 = (bf16[18,2,40,128]{3,2,1,0:T(8,128)(2,1)S(1)}, bf16[18,2,40,128]{3,2,1,0:T(8,128)(2,1)S(1)}, u32[]{:S(2)}, u32[]{:S(2)}) collective-permute-start(bf16[18,2,40,128]{3,2,1,0:T(8,128)(2,1)S(1)} %get-tuple-element.15), channel_id=1, source_target_pairs={{0,2},{2,4},{4,6},{6,8},{8,10},{10,12},{12,14},{14,16},{16,18},{18... | collective-permute-start | bytes 1105928 | tf_op jit(solution)/shard_map/ppermute | solution.py:390
  40.7 5.3 %collective-permute-start.5 = (bf16[18,2,40,128]{3,2,1,0:T(8,128)(2,1)S(1)}, bf16[18,2,40,128]{3,2,1,0:T(8,128)(2,1)S(1)}, u32[]{:S(2)}, u32[]{:S(2)}) collective-permute-start(bf16[18,2,40,128]{3,2,1,0:T(8,128)(2,1)S(1)} %get-tuple-element.16), channel_id=1, source_target_pairs={{2,0},{4,2},{6,4},{8,6},{10,8},{12,10},{14,12},{16,14},{18,16},{20... | collective-permute-start | bytes 1105928 | tf_op jit(solution)/shard_map/ppermute | solution.py:391
  46.0 2.9 %transport_first.2 = (f32[18,8,40,128]{3,2,1,0:T(8,128)S(1)}, bf16[18,2,40,128]{3,2,1,0:T(8,128)(2,1)S(1)}, bf16[18,2,40,128]{3,2,1,0:T(8,128)(2,1)S(1)}) custom-call(bf16[40,36,8,128]{3,2,1,0:T(8,128)(2,1)S(1)} %copy-done, bf16[36,8,128]{2,1,0:T(8,128)(2,1)S(1)} %copy-done.2, bf16[36,8,128]{2,1,0:T(8,128)(2,1)S(1)} %copy-done.3, bf16[256,128]{1,0:T(8,128)(2,1)S(1)} %copy-done.6), custom_call_target="tpu_custom_call" | custom-call | flops 29491200 | bytes 5898240 | tf_op jit(solution)/shard_map/transport_first/pallas_call | solution.py:174
  48.9 0.1 collective-permute-start
  48.9 6.9 %collective-permute-start.1 = (bf16[18,2,40,128]{3,2,1,0:T(8,128)(2,1)S(1)}, bf16[18,2,40,128]{3,2,1,0:T(8,128)(2,1)S(1)}, u32[]{:S(2)}, u32[]{:S(2)}) collective-permute-start(bf16[18,2,40,128]{3,2,1,0:T(8,128)(2,1)S(1)} %get-tuple-element.13), channel_id=1, source_target_pairs={{2,0},{4,2},{6,4},{8,6},{10,8},{12,10},{14,12},{16,14},{18,16},{20... | collective-permute-start | bytes 1105928 | tf_op jit(solution)/shard_map/ppermute | solution.py:391
  56.1 8.5 %collective-permute-done.2.refs_5_ = bf16[36,2,128]{2,1,0:T(2,128)(2,1)S(1)} collective-permute-done((bf16[36,2,128]{2,1,0:T(2,128)(2,1)S(1)}, bf16[36,2,128]{2,1,0:T(2,128)(2,1)S(1)}, u32[]{:S(2)}, u32[]{:S(2)}) %collective-permute-start.2) | collective-permute-done | bytes 18464 | tf_op jit(solution)/shard_map/ppermute | solution.py:380
  64.6 3.0 %collective-permute-done.3.refs_6_ = bf16[36,2,128]{2,1,0:T(2,128)(2,1)S(1)} collective-permute-done((bf16[36,2,128]{2,1,0:T(2,128)(2,1)S(1)}, bf16[36,2,128]{2,1,0:T(2,128)(2,1)S(1)}, u32[]{:S(2)}, u32[]{:S(2)}) %collective-permute-start.3) | collective-permute-done | bytes 18464 | tf_op jit(solution)/shard_map/ppermute | solution.py:381
  67.7 4.9 %transport_second.3.refs_1_ = bf16[18,3,128,128]{3,2,1,0:T(8,128)(2,1)S(1)} custom-call(f32[18,8,40,128]{3,2,1,0:T(8,128)S(1)} %get-tuple-element.14.refs_0_, bf16[18,2,40,128]{3,2,1,0:T(8,128)(2,1)S(1)} %collective-permute-done.4.refs_1_, bf16[18,2,40,128]{3,2,1,0:T(8,128)(2,1)S(1)} %collective-permute-done.5.refs_2_, bf16[36,8,128]{2,1,0:T(8,128)(2,1)S(1)} %copy-done.2, ...), custom_call_target="tpu_custom_call" | custom-call | flops 29491200 | bytes 5898240 | tf_op jit(solution)/shard_map/transport_second/pallas_call | solution.py:214
  72.5 3.8 %collective-permute-start.7 = (bf16[18,3,128,128]{3,2,1,0:T(8,128)(2,1)S(1)}, bf16[18,3,128,128]{3,2,1,0:T(8,128)(2,1)}, u32[]{:S(2)}, u32[]{:S(2)}) collective-permute-start(bf16[18,3,128,128]{3,2,1,0:T(8,128)(2,1)S(1)} %transport_second.3.refs_1_), channel_id=1, source_target_pairs={{0,1},{1,0},{2,3},{3,2},{4,5},{5,4},{6,7},{7,6},{8,9},{9,8},{10,11... | collective-permute-start | bytes 5308424 | tf_op jit(solution)/shard_map/ppermute | solution.py:396
  76.3 4.9 %transport_second.2.refs_0_ = bf16[18,3,128,128]{3,2,1,0:T(8,128)(2,1)S(1)} custom-call(f32[18,8,40,128]{3,2,1,0:T(8,128)S(1)} %get-tuple-element.11.refs_0_, bf16[18,2,40,128]{3,2,1,0:T(8,128)(2,1)S(1)} %collective-permute-done.refs_1_, bf16[18,2,40,128]{3,2,1,0:T(8,128)(2,1)S(1)} %collective-permute-done.1.refs_2_, bf16[36,8,128]{2,1,0:T(8,128)(2,1)S(1)} %copy-done.2, ...), custom_call_target="tpu_custom_call" | custom-call | flops 29491200 | bytes 5898240 | tf_op jit(solution)/shard_map/transport_second/pallas_call | solution.py:214
  81.2 0.1 collective-permute-start.6
  81.4 3.7 %collective-permute-done.6.refs_2_ = bf16[18,3,128,128]{3,2,1,0:T(8,128)(2,1)} collective-permute-done((bf16[18,3,128,128]{3,2,1,0:T(8,128)(2,1)S(1)}, bf16[18,3,128,128]{3,2,1,0:T(8,128)(2,1)}, u32[]{:S(2)}, u32[]{:S(2)}) %collective-permute-start.6) | collective-permute-done | bytes 1769504 | tf_op jit(solution)/shard_map/ppermute | solution.py:396
  85.1 23.1 %all-gather.3.cloned.1.call-done = bf16[640,4608]{1,0:T(8,128)(2,1)} async-done(((bf16[40,4608]{1,0:T(8,128)(2,1)}), bf16[640,4608]{1,0:T(8,128)(2,1)}) %all-gather.3.cloned.1.call-update) | async-done | bytes 5898256 | tf_op jit(solution)/shard_map/all_gather | solution.py:353
  108.2 29.6 %solve_columns.1 = bf16[40,36,8,128]{3,2,1,0:T(8,128)(2,1)} custom-call(s32[8,128]{1,0:T(8,128)S(1)} %fusion.3.pos_ref, bf16[18,3,128,128]{3,2,1,0:T(8,128)(2,1)S(1)} %transport_second.2.refs_0_, bf16[18,3,128,128]{3,2,1,0:T(8,128)(2,1)} %copy-done.1, bf16[18,3,128,128]{3,2,1,0:T(8,128)(2,1)} %collective-permute-done.6.refs_2_, ...), custom_call_target="tpu_custom_call" | custom-call | flops 212336640 | bytes 12582912 | tf_op jit(solution)/shard_map/solve_columns/pallas_call | solution.py:314
  (32 shorter events, 0.4 us)
Async XLA Ops:
  6.5 101.7 %all-gather.3.cloned.1.call-start = ((), (), s32[]{:S(2)}) async-start(), calls=%async_computation | async-start | bytes 6266880 | tf_op jit(solution)/shard_map/all_gather | solution.py:353
  7.9 14.2 %collective-permute-start.14 = (bf16[40,576]{1,0:T(8,128)(2,1)S(1)}, bf16[40,576]{1,0:T(8,128)(2,1)S(1)}, u32[]{:S(2)}, u32[]{:S(2)}) collective-permute-start(bf16[40,576]{1,0:T(8,128)(2,1)S(1)} %pad.4), channel_id=1, source_target_pairs={{14,0},{0,2},{2,4},{4,6},{6,8},{8,10},{10,12},{12,14},{30,16},{16,... | collective-permute-start | bytes 138248 | tf_op jit(solution)/shard_map/ppermute | solution.py:347
  10.4 14.1 %collective-permute-start.13 = (bf16[40,576]{1,0:T(8,128)(2,1)S(1)}, bf16[40,576]{1,0:T(8,128)(2,1)S(1)}, u32[]{:S(2)}, u32[]{:S(2)}) collective-permute-start(bf16[40,576]{1,0:T(8,128)(2,1)S(1)} %pad.4), channel_id=1, source_target_pairs={{12,0},{14,2},{0,4},{2,6},{4,8},{6,10},{8,12},{10,14},{28,16},{30,... | collective-permute-start | bytes 138248 | tf_op jit(solution)/shard_map/ppermute | solution.py:347
  13.4 11.8 %collective-permute-start.12 = (bf16[40,576]{1,0:T(8,128)(2,1)S(1)}, bf16[40,576]{1,0:T(8,128)(2,1)S(1)}, u32[]{:S(2)}, u32[]{:S(2)}) collective-permute-start(bf16[40,576]{1,0:T(8,128)(2,1)S(1)} %pad.4), channel_id=1, source_target_pairs={{10,0},{12,2},{14,4},{0,6},{2,8},{4,10},{6,12},{8,14},{26,16},{28,... | collective-permute-start | bytes 138248 | tf_op jit(solution)/shard_map/ppermute | solution.py:347
  17.2 8.1 %collective-permute-start.11 = (bf16[40,576]{1,0:T(8,128)(2,1)S(1)}, bf16[40,576]{1,0:T(8,128)(2,1)S(1)}, u32[]{:S(2)}, u32[]{:S(2)}) collective-permute-start(bf16[40,576]{1,0:T(8,128)(2,1)S(1)} %pad.4), channel_id=1, source_target_pairs={{8,0},{10,2},{12,4},{14,6},{0,8},{2,10},{4,12},{6,14},{24,16},{26,... | collective-permute-start | bytes 138248 | tf_op jit(solution)/shard_map/ppermute | solution.py:347
  17.6 7.6 %collective-permute-start.10 = (bf16[40,576]{1,0:T(8,128)(2,1)S(1)}, bf16[40,576]{1,0:T(8,128)(2,1)S(1)}, u32[]{:S(2)}, u32[]{:S(2)}) collective-permute-start(bf16[40,576]{1,0:T(8,128)(2,1)S(1)} %pad.4), channel_id=1, source_target_pairs={{6,0},{8,2},{10,4},{12,6},{14,8},{0,10},{2,12},{4,14},{22,16},{24,... | collective-permute-start | bytes 138248 | tf_op jit(solution)/shard_map/ppermute | solution.py:347
  22.1 8.2 %collective-permute-start.9 = (bf16[40,576]{1,0:T(8,128)(2,1)S(1)}, bf16[40,576]{1,0:T(8,128)(2,1)S(1)}, u32[]{:S(2)}, u32[]{:S(2)}) collective-permute-start(bf16[40,576]{1,0:T(8,128)(2,1)S(1)} %pad.4), channel_id=1, source_target_pairs={{4,0},{6,2},{8,4},{10,6},{12,8},{14,10},{0,12},{2,14},{20,16},{22,... | collective-permute-start | bytes 138248 | tf_op jit(solution)/shard_map/ppermute | solution.py:347
  24.5 6.2 %collective-permute-start.8 = (bf16[40,576]{1,0:T(8,128)(2,1)S(1)}, bf16[40,576]{1,0:T(8,128)(2,1)S(1)}, u32[]{:S(2)}, u32[]{:S(2)}) collective-permute-start(bf16[40,576]{1,0:T(8,128)(2,1)S(1)} %pad.4), channel_id=1, source_target_pairs={{2,0},{4,2},{6,4},{8,6},{10,8},{12,10},{14,12},{0,14},{18,16},{20,... | collective-permute-start | bytes 138248 | tf_op jit(solution)/shard_map/ppermute | solution.py:347
  31.7 1.8 %copy-start = (bf16[40,36,8,128]{3,2,1,0:T(8,128)(2,1)S(1)}, bf16[40,36,8,128]{3,2,1,0:T(8,128)(2,1)}, u32[]{:S(2)}) copy-start(bf16[40,36,8,128]{3,2,1,0:T(8,128)(2,1)} %refs_0_.3) | copy-start | bytes 8847364
  33.5 0.9 copy-start.2
  34.4 0.9 copy-start.3
  35.3 0.8 copy-start.6
  36.1 31.5 %copy-start.4 = (bf16[256,256]{1,0:T(8,128)(2,1)S(1)}, bf16[256,256]{1,0:T(8,128)(2,1)}, u32[]{:S(2)}) copy-start(bf16[256,256]{1,0:T(8,128)(2,1)} %constant.99.clone.refs_7_) | copy-start | bytes 393220
  36.1 31.5 %copy-start.5 = (bf16[128,256]{1,0:T(8,128)(2,1)S(1)}, bf16[128,256]{1,0:T(8,128)(2,1)}, u32[]{:S(2)}) copy-start(bf16[128,256]{1,0:T(8,128)(2,1)} %constant.100.clone.refs_8_) | copy-start | bytes 196612
  39.0 28.6 %collective-permute-start.4 = (bf16[18,2,40,128]{3,2,1,0:T(8,128)(2,1)S(1)}, bf16[18,2,40,128]{3,2,1,0:T(8,128)(2,1)S(1)}, u32[]{:S(2)}, u32[]{:S(2)}) collective-permute-start(bf16[18,2,40,128]{3,2,1,0:T(8,128)(2,1)S(1)} %get-tuple-element.15), channel_id=1, source_target_pairs={{0,2},{2,4},{4,6},{6,8},{8,10},{10,12},{12,14},{14,16},{16,18},{18... | collective-permute-start | bytes 1105928 | tf_op jit(solution)/shard_map/ppermute | solution.py:390
  40.7 27.0 %collective-permute-start.5 = (bf16[18,2,40,128]{3,2,1,0:T(8,128)(2,1)S(1)}, bf16[18,2,40,128]{3,2,1,0:T(8,128)(2,1)S(1)}, u32[]{:S(2)}, u32[]{:S(2)}) collective-permute-start(bf16[18,2,40,128]{3,2,1,0:T(8,128)(2,1)S(1)} %get-tuple-element.16), channel_id=1, source_target_pairs={{2,0},{4,2},{6,4},{8,6},{10,8},{12,10},{14,12},{16,14},{18,16},{20... | collective-permute-start | bytes 1105928 | tf_op jit(solution)/shard_map/ppermute | solution.py:391
  48.9 27.5 %collective-permute-start = (bf16[18,2,40,128]{3,2,1,0:T(8,128)(2,1)S(1)}, bf16[18,2,40,128]{3,2,1,0:T(8,128)(2,1)S(1)}, u32[]{:S(2)}, u32[]{:S(2)}) collective-permute-start(bf16[18,2,40,128]{3,2,1,0:T(8,128)(2,1)S(1)} %get-tuple-element.12), channel_id=1, source_target_pairs={{0,2},{2,4},{4,6},{6,8},{8,10},{10,12},{12,14},{14,16},{16,18},{18... | collective-permute-start | bytes 1105928 | tf_op jit(solution)/shard_map/ppermute | solution.py:390
  48.9 27.4 %collective-permute-start.1 = (bf16[18,2,40,128]{3,2,1,0:T(8,128)(2,1)S(1)}, bf16[18,2,40,128]{3,2,1,0:T(8,128)(2,1)S(1)}, u32[]{:S(2)}, u32[]{:S(2)}) collective-permute-start(bf16[18,2,40,128]{3,2,1,0:T(8,128)(2,1)S(1)} %get-tuple-element.13), channel_id=1, source_target_pairs={{2,0},{4,2},{6,4},{8,6},{10,8},{12,10},{14,12},{16,14},{18,16},{20... | collective-permute-start | bytes 1105928 | tf_op jit(solution)/shard_map/ppermute | solution.py:391
  55.9 8.7 %collective-permute-start.2 = (bf16[36,2,128]{2,1,0:T(2,128)(2,1)S(1)}, bf16[36,2,128]{2,1,0:T(2,128)(2,1)S(1)}, u32[]{:S(2)}, u32[]{:S(2)}) collective-permute-start(bf16[36,2,128]{2,1,0:T(2,128)(2,1)S(1)} %pad_maximum_fusion), channel_id=1, source_target_pairs={{0,2},{2,4},{4,6},{6,8},{8,10},{10,12},{12,14},{14,16},{16,18},{18... | collective-permute-start | bytes 55304 | tf_op jit(solution)/shard_map/ppermute | solution.py:380
  64.6 3.0 %collective-permute-start.3 = (bf16[36,2,128]{2,1,0:T(2,128)(2,1)S(1)}, bf16[36,2,128]{2,1,0:T(2,128)(2,1)S(1)}, u32[]{:S(2)}, u32[]{:S(2)}) collective-permute-start(bf16[36,2,128]{2,1,0:T(2,128)(2,1)S(1)} %pad_maximum_fusion.1), channel_id=1, source_target_pairs={{2,0},{4,2},{6,4},{8,6},{10,8},{12,10},{14,12},{16,14},{18,16},{20... | collective-permute-start | bytes 55304 | tf_op jit(solution)/shard_map/ppermute | solution.py:381
  72.5 35.7 %copy-start.1 = (bf16[18,3,128,128]{3,2,1,0:T(8,128)(2,1)}, bf16[18,3,128,128]{3,2,1,0:T(8,128)(2,1)S(1)}, u32[]{:S(2)}) copy-start(bf16[18,3,128,128]{3,2,1,0:T(8,128)(2,1)S(1)} %transport_second.3.refs_1_) | copy-start | bytes 5308420
  72.5 8.8 %copy-start.7 = (s32[1024,1]{0,1:T(1,128)S(1)}, s32[1024,1]{0,1:T(1,128)}, u32[]{:S(2)}) copy-start(s32[1024,1]{0,1:T(1,128)} %param.11) | copy-start | bytes 12292
  72.5 8.8 %collective-permute-start.7 = (bf16[18,3,128,128]{3,2,1,0:T(8,128)(2,1)S(1)}, bf16[18,3,128,128]{3,2,1,0:T(8,128)(2,1)}, u32[]{:S(2)}, u32[]{:S(2)}) collective-permute-start(bf16[18,3,128,128]{3,2,1,0:T(8,128)(2,1)S(1)} %transport_second.3.refs_1_), channel_id=1, source_target_pairs={{0,1},{1,0},{2,3},{3,2},{4,5},{5,4},{6,7},{7,6},{8,9},{9,8},{10,11... | collective-permute-start | bytes 5308424 | tf_op jit(solution)/shard_map/ppermute | solution.py:396
  81.2 3.9 %collective-permute-start.6 = (bf16[18,3,128,128]{3,2,1,0:T(8,128)(2,1)S(1)}, bf16[18,3,128,128]{3,2,1,0:T(8,128)(2,1)}, u32[]{:S(2)}, u32[]{:S(2)}) collective-permute-start(bf16[18,3,128,128]{3,2,1,0:T(8,128)(2,1)S(1)} %transport_second.2.refs_0_), channel_id=1, source_target_pairs={{0,1},{1,0},{2,3},{3,2},{4,5},{5,4},{6,7},{7,6},{8,9},{9,8},{10,11... | collective-permute-start | bytes 5308424 | tf_op jit(solution)/shard_map/ppermute | solution.py:396
Sparse Core Ops, SparseCore 0:
  31.8 76.3 all-gather.2

commit v3 on v2

--- a/solution.py
+++ b/solution.py
@@ -16,6 +16,7 @@
 LANES = 128
 TRIPLES = ((0, 1, 2), (3, 4, 5), (6, 7))
 HEIGHT = 48
+DEPTH = 80
 F32, BF16 = jnp.float32, jnp.bfloat16
 
 
@@ -233,54 +234,96 @@
     )(state, left, right, wind_x, wind_y, wind_l, wind_r, table, mean)
 
 
-def solve_kernel(n_fields, n_pieces, pos_ref, *refs):
-    fields = refs[:n_fields]
-    pieces = refs[n_fields : n_fields + n_pieces]
-    out_ref = refs[n_fields + n_pieces]
-    matrices, value, result, final = refs[n_fields + n_pieces + 1 :]
+def align_kernel(n_fields, *refs):
+    fields, out_ref, scratch = refs[:n_fields], refs[n_fields], refs[n_fields + 1]
+    width_y = fields[0].shape[2]
+    level = 0
+    for field in fields:
+        for l in range(field.shape[0]):
+            scratch[pl.ds(level, width_y, stride=DEPTH), :] = field[l, 0].astype(F32)
+            level += 1
+    for l in range(level, DEPTH):
+        scratch[pl.ds(l, width_y, stride=DEPTH), :] = jnp.zeros((width_y, LANES), F32)
+
+    @pl.loop(0, width_y, unroll=8)
+    def _(y):
+        rows = pl.ds(pl.multiple_of(y * DEPTH, DEPTH), DEPTH)
+        out_ref[0, rows, :] = scratch[rows, :].astype(BF16)
+
+
+def align(fields):
+    _, triples, width_y, lanes = fields[0].shape
+    return pl.pallas_call(
+        functools.partial(align_kernel, len(fields)),
+        grid=(triples,),
+        in_specs=[
+            pl.BlockSpec((f.shape[0], 1, width_y, lanes), lambda g: (0, g, 0, 0)) for f in fields
+        ],
+        out_specs=pl.BlockSpec((1, width_y * DEPTH, lanes), lambda g: (g, 0, 0)),
+        out_shape=jax.ShapeDtypeStruct((triples, width_y * DEPTH, lanes), BF16),
+        scratch_shapes=[pltpu.VMEM((width_y * DEPTH, lanes), F32)],
+        compiler_params=pltpu.CompilerParams(vmem_limit_bytes=24 << 20),
+        cost_estimate=pl.CostEstimate(flops=1000, bytes_accessed=1000, transcendentals=0),
+        name="align_columns",
+    )(*fields)
+
+
+def lanes_from(ref, k, rows, start):
+    tile, shift = divmod(start, LANES)
+    part = ref[k, rows, tile * LANES : (tile + 1) * LANES].astype(F32)
+    if shift:
+        part = pltpu.roll(part, LANES - shift, axis=1)
+        if (tile + 2) * LANES <= ref.shape[2]:
+            after = ref[k, rows, (tile + 1) * LANES : (tile + 2) * LANES].astype(F32)
+            after = pltpu.roll(after, LANES - shift, axis=1)
+            lane = lax.broadcasted_iota(jnp.int32, part.shape, 1)
+            part = jnp.where(lane < LANES - shift, part, after)
+    return part
+
+
+def solve_kernel(
+    pos_ref, value_hbm, block_hbm, out_ref,
+    value_ref, block_ref, matrices, result, final, value_sem, block_sem,
+):
     groups, rows, width_x, width_y = out_ref.shape
-    levels = value.shape[0] // width_y
-    per_block = pieces[0].shape[2] // levels
-
-    base = 0
-    for piece in pieces:
-        count = piece.shape[0]
-
-        @pl.loop(0, count)
-        def _(k, piece=piece, base=base):
-            for j in range(per_block):
-                tile, shift = divmod(j * levels, LANES)
-                part = piece[k, :, tile * LANES : (tile + 1) * LANES].astype(F32)
-                if shift:
-                    part = pltpu.roll(part, LANES - shift, axis=1)
-                if shift + levels > LANES:
-                    after = piece[k, :, (tile + 1) * LANES : (tile + 2) * LANES].astype(F32)
-                    after = pltpu.roll(after, LANES - shift, axis=1)
-                    lane = lax.broadcasted_iota(jnp.int32, after.shape, 1)
-                    part = jnp.where(lane < LANES - shift, part, after)
-                matrices[(base + k) * per_block + j, : part.shape[0]] = part.astype(BF16)
-
-        base += count
-
+    levels = 2 * rows
+
+    count, _, lanes = block_ref.shape
+
+    def block_copy(k):
+        return pltpu.make_async_copy(block_hbm.at[k], block_ref.at[k], block_sem.at[k])
+
+    for k in range(count):
+        block_copy(k).start()
+    value_copy = pltpu.make_async_copy(value_hbm, value_ref, value_sem)
+    value_copy.start()
+    per_block = lanes // levels
+    tall = -(-rows // 8) * 8
+
+    @pl.loop(0, count)
+    def _(k):
+        block_copy(k).wait()
+        for j in range(per_block):
+            part = lanes_from(block_ref, k, slice(0, tall), j * levels)
+            matrices[2 * k * per_block + j, :tall] = part.astype(BF16)
+            part = lanes_from(block_ref, k, slice(2 * rows - tall, 2 * rows), j * levels)
+            part = pltpu.roll(part, rows, axis=0)
+            matrices[(2 * k + 1) * per_block + j, :tall] = part.astype(BF16)
+
+    value_copy.wait()
     lane = lax.broadcasted_iota(jnp.int32, (rows, LANES), 1)
     eye = (
         lax.broadcasted_iota(jnp.int32, (LANES, LANES), 0)
         == lax.broadcasted_iota(jnp.int32, (LANES, LANES), 1)
     ).astype(F32).astype(BF16)
     for g, triple in enumerate(TRIPLES):
-        level = 0
-        for field in fields:
-            for l in range(field.shape[0]):
-                value[pl.ds(level, width_y, stride=levels), :] = field[l, g].astype(F32)
-                level += 1
 
         @pl.loop(0, width_y, unroll=16)
-        def _(y, triple=triple):
-            start = pl.multiple_of(y * levels, 8)
-            columns = value[pl.ds(start, levels), :]
+        def _(y, g=g, triple=triple):
+            columns = value_ref[g, pl.ds(pl.multiple_of(y * DEPTH, DEPTH), DEPTH), :]
             columns = jnp.concatenate(
-                [columns, jnp.zeros((LANES - levels, LANES), F32)], axis=0
-            ).astype(BF16)
+                [columns, jnp.zeros((LANES - DEPTH, LANES), BF16)], axis=0
+            )
             chosen = jnp.concatenate([matrices[pos_ref[x, y]] for x in triple], axis=0)
             product = jnp.dot(chosen, columns, preferred_element_type=F32)
             picked = product[(len(triple) - 1) * HEIGHT :][:rows]
@@ -293,9 +336,11 @@
         @pl.loop(0, rows, unroll=12)
         def _(a, triple=triple):
             start = pl.multiple_of(a * width_y, width_y)
-            solved = result[pl.ds(start, width_y), :].astype(BF16)
             turned = lax.dot_general(
-                eye, solved, (((1,), (1,)), ((), ())), preferred_element_type=F32
+                eye,
+                result[pl.ds(start, width_y), :].astype(BF16),
+                (((1,), (1,)), ((), ())),
+                preferred_element_type=F32,
             )
             for i, x in enumerate(triple):
                 final[a, pl.ds(x, groups, stride=width_x), :] = turned[
@@ -307,30 +352,32 @@
         out_ref[:, a] = final[a].reshape(groups, width_x, width_y).astype(BF16)
 
 
-def solve(fields, pieces, position, groups, levels_out, width_x, width_y):
-    levels = sum(f.shape[0] for f in fields)
-    spans = sum(p.shape[0] * p.shape[2] for p in pieces) // levels
-    vmem = pl.BlockSpec(memory_space=pltpu.VMEM)
+def solve(value, block, position, shape):
+    groups, rows, width_x, width_y = shape
+    spans = 2 * block.shape[0] * (block.shape[2] // (2 * rows))
+    anywhere = pl.BlockSpec(memory_space=pl.ANY)
     return pl.pallas_call(
-        functools.partial(solve_kernel, len(fields), len(pieces)),
-        in_specs=[pl.BlockSpec(memory_space=pltpu.SMEM)]
-        + [vmem] * (len(fields) + len(pieces)),
-        out_specs=vmem,
-        out_shape=jax.ShapeDtypeStruct((groups, levels_out, width_x, width_y), BF16),
+        solve_kernel,
+        in_specs=[pl.BlockSpec(memory_space=pltpu.SMEM), anywhere, anywhere],
+        out_specs=pl.BlockSpec(memory_space=pltpu.VMEM),
+        out_shape=jax.ShapeDtypeStruct(shape, BF16),
         scratch_shapes=[
+            pltpu.VMEM(value.shape, BF16),
+            pltpu.VMEM(block.shape, BF16),
             pltpu.VMEM((spans, HEIGHT, LANES), BF16),
-            pltpu.VMEM((width_y * levels, LANES), F32),
-            pltpu.VMEM((levels_out * width_y, LANES), F32),
-            pltpu.VMEM((levels_out, groups * width_x, width_y), F32),
-        ],
-        compiler_params=pltpu.CompilerParams(vmem_limit_bytes=52 << 20),
+            pltpu.VMEM((rows * width_y, LANES), F32),
+            pltpu.VMEM((rows, groups * width_x, width_y), F32),
+            pltpu.SemaphoreType.DMA(()),
+            pltpu.SemaphoreType.DMA((block.shape[0],)),
+        ],
+        compiler_params=pltpu.CompilerParams(vmem_limit_bytes=58 << 20),
         cost_estimate=pl.CostEstimate(
-            flops=2 * levels_out * levels * groups * width_x * width_y,
+            flops=4 * rows * rows * groups * width_x * width_y,
             bytes_accessed=12 << 20,
             transcendentals=0,
         ),
         name="solve_columns",
-    )(position, *fields, *pieces)
+    )(position, value, block)
 
 
 def elem_index(y, x, z):
@@ -349,8 +396,9 @@
 
 def gather_matrices(block):
     near = [block] + [fetch(block, dz=d) for d in range(1, NZ_CHIPS)]
-    part = jnp.concatenate(near, axis=1)
-    return [lax.all_gather(part, ("y", "x"), axis=0)]
+    half = NZ_CHIPS // 2
+    halves = [jnp.concatenate(near[i : i + half], axis=1) for i in (0, half)]
+    return lax.all_gather(jnp.concatenate(halves, axis=0), ("y", "x"), axis=0)
 
 
 def span_position(span_ids, per_dev):
@@ -373,8 +421,7 @@
     other = lax.dynamic_slice_in_dim(mine, (1 - lev) * half_levels, half_levels, 2)
     block = jnp.concatenate([own, other], axis=2).transpose(1, 0, 2)
     block = block.reshape(half_levels, -1)
-    block = jnp.pad(block, ((0, -half_levels % 8), (0, 0)))
-    pieces = gather_matrices(block)
+    matrices = gather_matrices(block)
     position = span_position(span_of[:, 0], per_dev).reshape(width_x, width_y)
 
     wind_l = lax.ppermute(jnp.stack([wind_x[:, -1], wind_y[:, -1]], 1), ELEM, up)
@@ -394,9 +441,8 @@
         )
         own_fields.append(field)
         other_fields.append(lax.ppermute(field, "lev", [(0, 1), (1, 0)]))
-    return solve(
-        own_fields + other_fields, pieces, position, groups, half_levels, width_x, width_y
-    )
+    value = align(own_fields + other_fields)
+    return solve(value, matrices, position, tracers.shape)
 
 
 def solution(mesh):

time: 145 us -> 134 us (0.924)
  waiting for transfers between devices: 43.9 us -> 22.5 us
  Pallas kernels: 45.1 us -> 50.5 us
  local copies, waits for them, and re-layouts: 6.66 us -> 9.03 us
    all_gather x1, waiting for transfers between devices: 23.1 us -> 3.84 us  [gather_matrices(): return lax.all_gather(jnp.concatenate(halves, axis=0), ('y', 'x'), axis=0)]
    pallas_call x1 -> x2, Pallas kernels: 29.6 us -> 35 us  [the longest x1 24.6 us: solve(): pl.pallas_call(solve_kernel, in_specs=[pl.BlockSpec(memory_space=pltpu.SM...]
    unnamed x16, local copies, waits for them, and re-layouts: 4.45 us -> 7.5 us
    ppermute x2, starting transfers between devices: 12.2 us -> 13.9 us  [body(): right = lax.ppermute(to_left, ELEM, down)]
    ppermute x2, starting transfers between devices: 3.91 us -> 5.54 us  [body(): other_fields.append(lax.ppermute(field, 'lev', [(0, 1), (1, 0)]))]
    ppermute x7, waiting for transfers between devices: 5.49 us -> 3.91 us  [fetch(): return lax.ppermute(value, ELEM, pairs)]
  transfers between devices with their start and end apart: 16 -> 16, of which waited for: 6 -> 6; matrix products, arithmetic and copies ran while one was open for 0% -> 1% of each run, Pallas kernels for 11% -> 19%
where the time goes in v3:
time: 134 us
  Pallas kernels  50.5 us (38%)
  starting transfers between devices  36.7 us (27%)
  waiting for transfers between devices  22.5 us (17%)
  between operations  13.6 us (10%)
  local copies, waits for them, and re-layouts  9.03 us (7%)
  other arithmetic  1.6 us (1%)
    pallas_call x1, Pallas kernels, solve(): pl.pallas_call(solve_kernel, in_specs=[pl.BlockSpec(memory_space=pltpu.SM...  24.6 us
    ppermute x7, starting transfers between devices, fetch(): return lax.ppermute(value, ELEM, pairs)  16.1 us
    ppermute x2, starting transfers between devices, body(): right = lax.ppermute(to_left, ELEM, down)  13.9 us
    pallas_call x1, Pallas kernels, align(): pl.pallas_call(functools.partial(align_kernel, len(fields)), grid=(triple...  10.4 us
    pallas_call x2, Pallas kernels, second_part(): pl.pallas_call(lambda *refs: second_kernel(step, *refs), grid=(count // s...  9.72 us
    ppermute x1, waiting for transfers between devices, body(): lax.ppermute(jnp.stack([wind_x[:, -1], wind_y[:, -1]], 1), ELEM, up)  8.53 us
    unnamed x16, local copies, waits for them, and re-layouts  7.5 us
    pallas_call x2, Pallas kernels, first_part(): pl.pallas_call(lambda *refs: first_kernel(step, *refs), grid=(count // st...  5.74 us
  transfers between devices with their start and end apart: 16, of which 6 were waited for; matrix products, arithmetic and copies ran while one was open for 1% of the time, Pallas kernels for 19%

profile of v3, /device:TPU:1, one launch (start us, length us, event | category | flops | bytes accessed | tf_op | source)
XLA Modules:
  0.0 133.8 jit_solution(12857500115473016990)
XLA Ops:
  6.5 1.1 constant_dynamic-slice_fusion.1
  7.9 6.5 %collective-permute-start.8 = (bf16[36,576]{1,0:T(8,128)(2,1)S(1)}, bf16[36,576]{1,0:T(8,128)(2,1)S(1)}, u32[]{:S(2)}, u32[]{:S(2)}) collective-permute-start(bf16[36,576]{1,0:T(8,128)(2,1)S(1)} %reshape.5), channel_id=1, source_target_pairs={{2,0},{4,2},{6,4},{8,6},{10,8},{12,10},{14,12},{0,14},{18,16},{20,... | collective-permute-start | bytes 124424 | tf_op jit(solution)/shard_map/ppermute | solution.py:394
  14.4 1.2 collective-permute-start.9
  15.5 0.4 collective-permute-start.11
  15.9 4.6 %collective-permute-start.10 = (bf16[36,576]{1,0:T(8,128)(2,1)S(1)}, bf16[36,576]{1,0:T(8,128)(2,1)S(1)}, u32[]{:S(2)}, u32[]{:S(2)}) collective-permute-start(bf16[36,576]{1,0:T(8,128)(2,1)S(1)} %reshape.5), channel_id=1, source_target_pairs={{6,0},{8,2},{10,4},{12,6},{14,8},{0,10},{2,12},{4,14},{22,16},{24,... | collective-permute-start | bytes 124424 | tf_op jit(solution)/shard_map/ppermute | solution.py:394
  20.5 2.2 %collective-permute-start.13 = (bf16[36,576]{1,0:T(8,128)(2,1)S(1)}, bf16[36,576]{1,0:T(8,128)(2,1)S(1)}, u32[]{:S(2)}, u32[]{:S(2)}) collective-permute-start(bf16[36,576]{1,0:T(8,128)(2,1)S(1)} %reshape.5), channel_id=1, source_target_pairs={{12,0},{14,2},{0,4},{2,6},{4,8},{6,10},{8,12},{10,14},{28,16},{30,... | collective-permute-start | bytes 124424 | tf_op jit(solution)/shard_map/ppermute | solution.py:394
  22.6 1.4 %collective-permute-start.14 = (bf16[36,576]{1,0:T(8,128)(2,1)S(1)}, bf16[36,576]{1,0:T(8,128)(2,1)S(1)}, u32[]{:S(2)}, u32[]{:S(2)}) collective-permute-start(bf16[36,576]{1,0:T(8,128)(2,1)S(1)} %reshape.5), channel_id=1, source_target_pairs={{14,0},{0,2},{2,4},{4,6},{6,8},{8,10},{10,12},{12,14},{30,16},{16,... | collective-permute-start | bytes 124424 | tf_op jit(solution)/shard_map/ppermute | solution.py:394
  24.0 0.1 concatenate.13
  24.2 2.3 %collective-permute-done.12 = bf16[36,576]{1,0:T(8,128)(2,1)S(1)} collective-permute-done((bf16[36,576]{1,0:T(8,128)(2,1)S(1)}, bf16[36,576]{1,0:T(8,128)(2,1)S(1)}, u32[]{:S(2)}, u32[]{:S(2)}) %collective-permute-start.12) | collective-permute-done | bytes 41504 | tf_op jit(solution)/shard_map/ppermute | solution.py:394
  26.4 1.6 %collective-permute-done.13 = bf16[36,576]{1,0:T(8,128)(2,1)S(1)} collective-permute-done((bf16[36,576]{1,0:T(8,128)(2,1)S(1)}, bf16[36,576]{1,0:T(8,128)(2,1)S(1)}, u32[]{:S(2)}, u32[]{:S(2)}) %collective-permute-start.13) | collective-permute-done | bytes 41504 | tf_op jit(solution)/shard_map/ppermute | solution.py:394
  28.1 0.1 concatenate.14
  28.2 0.8 pad_maximum_fusion
  29.0 1.8 %copy-done.1 = bf16[40,36,8,128]{3,2,1,0:T(8,128)(2,1)S(1)} copy-done((bf16[40,36,8,128]{3,2,1,0:T(8,128)(2,1)S(1)}, bf16[40,36,8,128]{3,2,1,0:T(8,128)(2,1)}, u32[]{:S(2)}) %copy-start.1) | copy-done | bytes 2949144
  30.8 0.9 copy-done.2
  31.7 0.9 copy-done.3
  32.6 0.8 copy-done.6
  33.5 2.9 %transport_first.2 = (f32[18,8,40,128]{3,2,1,0:T(8,128)S(1)}, bf16[18,2,40,128]{3,2,1,0:T(8,128)(2,1)S(1)}, bf16[18,2,40,128]{3,2,1,0:T(8,128)(2,1)S(1)}) custom-call(bf16[40,36,8,128]{3,2,1,0:T(8,128)(2,1)S(1)} %copy-done.1, bf16[36,8,128]{2,1,0:T(8,128)(2,1)S(1)} %copy-done.2, bf16[36,8,128]{2,1,0:T(8,128)(2,1)S(1)} %copy-done.3, ...), custom_call_target="tpu_custom_call" | custom-call | flops 29491200 | bytes 5898240 | tf_op jit(solution)/shard_map/transport_first/pallas_call | solution.py:175
  36.3 1.0 collective-permute-start
  37.3 7.0 %collective-permute-start.1 = (bf16[18,2,40,128]{3,2,1,0:T(8,128)(2,1)S(1)}, bf16[18,2,40,128]{3,2,1,0:T(8,128)(2,1)S(1)}, u32[]{:S(2)}, u32[]{:S(2)}) collective-permute-start(bf16[18,2,40,128]{3,2,1,0:T(8,128)(2,1)S(1)} %get-tuple-element.13), channel_id=1, source_target_pairs={{2,0},{4,2},{6,4},{8,6},{10,8},{12,10},{14,12},{16,14},{18,16},{20... | collective-permute-start | bytes 1105928 | tf_op jit(solution)/shard_map/ppermute | solution.py:438
  44.3 2.9 %transport_first.3 = (f32[18,8,40,128]{3,2,1,0:T(8,128)S(1)}, bf16[18,2,40,128]{3,2,1,0:T(8,128)(2,1)S(1)}, bf16[18,2,40,128]{3,2,1,0:T(8,128)(2,1)S(1)}) custom-call(bf16[40,36,8,128]{3,2,1,0:T(8,128)(2,1)S(1)} %copy-done.1, bf16[36,8,128]{2,1,0:T(8,128)(2,1)S(1)} %copy-done.2, bf16[36,8,128]{2,1,0:T(8,128)(2,1)S(1)} %copy-done.3, ...), custom_call_target="tpu_custom_call" | custom-call | flops 29491200 | bytes 5898240 | tf_op jit(solution)/shard_map/transport_first/pallas_call | solution.py:175
  47.2 6.9 %collective-permute-start.5 = (bf16[18,2,40,128]{3,2,1,0:T(8,128)(2,1)S(1)}, bf16[18,2,40,128]{3,2,1,0:T(8,128)(2,1)S(1)}, u32[]{:S(2)}, u32[]{:S(2)}) collective-permute-start(bf16[18,2,40,128]{3,2,1,0:T(8,128)(2,1)S(1)} %get-tuple-element.16), channel_id=1, source_target_pairs={{2,0},{4,2},{6,4},{8,6},{10,8},{12,10},{14,12},{16,14},{18,16},{20... | collective-permute-start | bytes 1105928 | tf_op jit(solution)/shard_map/ppermute | solution.py:438
  54.4 8.5 %collective-permute-done.2.refs_5_ = bf16[36,2,128]{2,1,0:T(2,128)(2,1)S(1)} collective-permute-done((bf16[36,2,128]{2,1,0:T(2,128)(2,1)S(1)}, bf16[36,2,128]{2,1,0:T(2,128)(2,1)S(1)}, u32[]{:S(2)}, u32[]{:S(2)}) %collective-permute-start.2) | collective-permute-done | bytes 18464 | tf_op jit(solution)/shard_map/ppermute | solution.py:427
  62.9 3.0 %collective-permute-done.3.refs_6_ = bf16[36,2,128]{2,1,0:T(2,128)(2,1)S(1)} collective-permute-done((bf16[36,2,128]{2,1,0:T(2,128)(2,1)S(1)}, bf16[36,2,128]{2,1,0:T(2,128)(2,1)S(1)}, u32[]{:S(2)}, u32[]{:S(2)}) %collective-permute-start.3) | collective-permute-done | bytes 18464 | tf_op jit(solution)/shard_map/ppermute | solution.py:428
  65.9 4.9 %transport_second.2.refs_0_ = bf16[18,3,128,128]{3,2,1,0:T(8,128)(2,1)S(1)} custom-call(f32[18,8,40,128]{3,2,1,0:T(8,128)S(1)} %get-tuple-element.11.refs_0_, bf16[18,2,40,128]{3,2,1,0:T(8,128)(2,1)S(1)} %collective-permute-done.refs_1_, bf16[18,2,40,128]{3,2,1,0:T(8,128)(2,1)S(1)} %collective-permute-done.1.refs_2_, bf16[36,8,128]{2,1,0:T(8,128)(2,1)S(1)} %copy-done.2, ...), custom_call_target="tpu_custom_call" | custom-call | flops 29491200 | bytes 5898240 | tf_op jit(solution)/shard_map/transport_second/pallas_call | solution.py:215
  70.8 5.4 %collective-permute-start.6 = (bf16[18,3,128,128]{3,2,1,0:T(8,128)(2,1)S(1)}, bf16[18,3,128,128]{3,2,1,0:T(8,128)(2,1)}, u32[]{:S(2)}, u32[]{:S(2)}) collective-permute-start(bf16[18,3,128,128]{3,2,1,0:T(8,128)(2,1)S(1)} %transport_second.2.refs_0_), channel_id=1, source_target_pairs={{0,1},{1,0},{2,3},{3,2},{4,5},{5,4},{6,7},{7,6},{8,9},{9,8},{10,11... | collective-permute-start | bytes 5308424 | tf_op jit(solution)/shard_map/ppermute | solution.py:443
  76.3 4.8 %transport_second.3.refs_1_ = bf16[18,3,128,128]{3,2,1,0:T(8,128)(2,1)S(1)} custom-call(f32[18,8,40,128]{3,2,1,0:T(8,128)S(1)} %get-tuple-element.14.refs_0_, bf16[18,2,40,128]{3,2,1,0:T(8,128)(2,1)S(1)} %collective-permute-done.4.refs_1_, bf16[18,2,40,128]{3,2,1,0:T(8,128)(2,1)S(1)} %collective-permute-done.5.refs_2_, bf16[36,8,128]{2,1,0:T(8,128)(2,1)S(1)} %copy-done.2, ...), custom_call_target="tpu_custom_call" | custom-call | flops 29491200 | bytes 5898240 | tf_op jit(solution)/shard_map/transport_second/pallas_call | solution.py:215
  81.2 0.6 fusion.3.pos_ref
  81.9 3.2 %collective-permute-done.7.refs_3_ = bf16[18,3,128,128]{3,2,1,0:T(8,128)(2,1)} collective-permute-done((bf16[18,3,128,128]{3,2,1,0:T(8,128)(2,1)S(1)}, bf16[18,3,128,128]{3,2,1,0:T(8,128)(2,1)}, u32[]{:S(2)}, u32[]{:S(2)}) %collective-permute-start.7) | collective-permute-done | bytes 1769504 | tf_op jit(solution)/shard_map/ppermute | solution.py:443
  85.0 10.4 %align_columns.1.value_hbm = bf16[3,10240,128]{2,1,0:T(8,128)(2,1)S(1)} custom-call(bf16[18,3,128,128]{3,2,1,0:T(8,128)(2,1)S(1)} %transport_second.2.refs_0_, bf16[18,3,128,128]{3,2,1,0:T(8,128)(2,1)S(1)} %transport_second.3.refs_1_, bf16[18,3,128,128]{3,2,1,0:T(8,128)(2,1)} %collective-permute-done.6.refs_2_, ...), custom_call_target="tpu_custom_call" | custom-call | flops 1000 | bytes 1000 | tf_op jit(solution)/shard_map/align_columns/pallas_call | solution.py:256
  95.5 3.0 %copy-done = bf16[3,10240,128]{2,1,0:T(8,128)(2,1)} copy-done((bf16[3,10240,128]{2,1,0:T(8,128)(2,1)}, bf16[3,10240,128]{2,1,0:T(8,128)(2,1)S(1)}, u32[]{:S(2)}) %copy-start) | copy-done | bytes 7864344
  98.5 3.8 %all-gather.3.cloned.1.call-done = bf16[1152,2304]{1,0:T(8,128)(2,1)} async-done(((bf16[72,2304]{1,0:T(8,128)(2,1)}), bf16[1152,2304]{1,0:T(8,128)(2,1)}) %all-gather.3.cloned.1.call-update) | async-done | bytes 5308432 | tf_op jit(solution)/shard_map/all_gather | solution.py:401
  102.4 24.6 %solve_columns.1 = bf16[40,36,8,128]{3,2,1,0:T(8,128)(2,1)} custom-call(s32[8,128]{1,0:T(8,128)} %fusion.3.pos_ref, bf16[3,10240,128]{2,1,0:T(8,128)(2,1)} %copy-done, bf16[16,72,2304]{2,1,0:T(8,128)(2,1)} %bitcast.4), custom_call_target="tpu_custom_call" | custom-call | flops 212336640 | bytes 12582912 | tf_op jit(solution)/shard_map/solve_columns/pallas_call | solution.py:359
  (34 shorter events, 0.8 us)
Async XLA Ops:
  6.5 95.8 %all-gather.3.cloned.1.call-start = ((), (), s32[]{:S(2)}) async-start(), calls=%async_computation | async-start | bytes 5640192 | tf_op jit(solution)/shard_map/all_gather | solution.py:401
  7.9 12.6 %collective-permute-start.8 = (bf16[36,576]{1,0:T(8,128)(2,1)S(1)}, bf16[36,576]{1,0:T(8,128)(2,1)S(1)}, u32[]{:S(2)}, u32[]{:S(2)}) collective-permute-start(bf16[36,576]{1,0:T(8,128)(2,1)S(1)} %reshape.5), channel_id=1, source_target_pairs={{2,0},{4,2},{6,4},{8,6},{10,8},{12,10},{14,12},{0,14},{18,16},{20,... | collective-permute-start | bytes 124424 | tf_op jit(solution)/shard_map/ppermute | solution.py:394
  14.4 8.3 %collective-permute-start.9 = (bf16[36,576]{1,0:T(8,128)(2,1)S(1)}, bf16[36,576]{1,0:T(8,128)(2,1)S(1)}, u32[]{:S(2)}, u32[]{:S(2)}) collective-permute-start(bf16[36,576]{1,0:T(8,128)(2,1)S(1)} %reshape.5), channel_id=1, source_target_pairs={{4,0},{6,2},{8,4},{10,6},{12,8},{14,10},{0,12},{2,14},{20,16},{22,... | collective-permute-start | bytes 124424 | tf_op jit(solution)/shard_map/ppermute | solution.py:394
  15.5 8.6 %collective-permute-start.11 = (bf16[36,576]{1,0:T(8,128)(2,1)S(1)}, bf16[36,576]{1,0:T(8,128)(2,1)S(1)}, u32[]{:S(2)}, u32[]{:S(2)}) collective-permute-start(bf16[36,576]{1,0:T(8,128)(2,1)S(1)} %reshape.5), channel_id=1, source_target_pairs={{8,0},{10,2},{12,4},{14,6},{0,8},{2,10},{4,12},{6,14},{24,16},{26,... | collective-permute-start | bytes 124424 | tf_op jit(solution)/shard_map/ppermute | solution.py:394
  15.9 8.1 %collective-permute-start.10 = (bf16[36,576]{1,0:T(8,128)(2,1)S(1)}, bf16[36,576]{1,0:T(8,128)(2,1)S(1)}, u32[]{:S(2)}, u32[]{:S(2)}) collective-permute-start(bf16[36,576]{1,0:T(8,128)(2,1)S(1)} %reshape.5), channel_id=1, source_target_pairs={{6,0},{8,2},{10,4},{12,6},{14,8},{0,10},{2,12},{4,14},{22,16},{24,... | collective-permute-start | bytes 124424 | tf_op jit(solution)/shard_map/ppermute | solution.py:394
  20.5 6.0 %collective-permute-start.12 = (bf16[36,576]{1,0:T(8,128)(2,1)S(1)}, bf16[36,576]{1,0:T(8,128)(2,1)S(1)}, u32[]{:S(2)}, u32[]{:S(2)}) collective-permute-start(bf16[36,576]{1,0:T(8,128)(2,1)S(1)} %reshape.5), channel_id=1, source_target_pairs={{10,0},{12,2},{14,4},{0,6},{2,8},{4,10},{6,12},{8,14},{26,16},{28,... | collective-permute-start | bytes 124424 | tf_op jit(solution)/shard_map/ppermute | solution.py:394
  20.5 7.6 %collective-permute-start.13 = (bf16[36,576]{1,0:T(8,128)(2,1)S(1)}, bf16[36,576]{1,0:T(8,128)(2,1)S(1)}, u32[]{:S(2)}, u32[]{:S(2)}) collective-permute-start(bf16[36,576]{1,0:T(8,128)(2,1)S(1)} %reshape.5), channel_id=1, source_target_pairs={{12,0},{14,2},{0,4},{2,6},{4,8},{6,10},{8,12},{10,14},{28,16},{30,... | collective-permute-start | bytes 124424 | tf_op jit(solution)/shard_map/ppermute | solution.py:394
  22.6 5.4 %collective-permute-start.14 = (bf16[36,576]{1,0:T(8,128)(2,1)S(1)}, bf16[36,576]{1,0:T(8,128)(2,1)S(1)}, u32[]{:S(2)}, u32[]{:S(2)}) collective-permute-start(bf16[36,576]{1,0:T(8,128)(2,1)S(1)} %reshape.5), channel_id=1, source_target_pairs={{14,0},{0,2},{2,4},{4,6},{6,8},{8,10},{10,12},{12,14},{30,16},{16,... | collective-permute-start | bytes 124424 | tf_op jit(solution)/shard_map/ppermute | solution.py:394
  29.0 1.8 %copy-start.1 = (bf16[40,36,8,128]{3,2,1,0:T(8,128)(2,1)S(1)}, bf16[40,36,8,128]{3,2,1,0:T(8,128)(2,1)}, u32[]{:S(2)}) copy-start(bf16[40,36,8,128]{3,2,1,0:T(8,128)(2,1)} %refs_0_.3) | copy-start | bytes 8847364
  30.8 0.9 copy-start.2
  31.7 0.9 copy-start.3
  32.6 0.8 copy-start.6
  33.4 32.5 %copy-start.4 = (bf16[256,256]{1,0:T(8,128)(2,1)S(1)}, bf16[256,256]{1,0:T(8,128)(2,1)}, u32[]{:S(2)}) copy-start(bf16[256,256]{1,0:T(8,128)(2,1)} %constant.97.clone.refs_7_) | copy-start | bytes 393220
  33.5 32.5 %copy-start.5 = (bf16[128,256]{1,0:T(8,128)(2,1)S(1)}, bf16[128,256]{1,0:T(8,128)(2,1)}, u32[]{:S(2)}) copy-start(bf16[128,256]{1,0:T(8,128)(2,1)} %constant.98.clone.refs_8_) | copy-start | bytes 196612
  36.3 29.6 %collective-permute-start = (bf16[18,2,40,128]{3,2,1,0:T(8,128)(2,1)S(1)}, bf16[18,2,40,128]{3,2,1,0:T(8,128)(2,1)S(1)}, u32[]{:S(2)}, u32[]{:S(2)}) collective-permute-start(bf16[18,2,40,128]{3,2,1,0:T(8,128)(2,1)S(1)} %get-tuple-element.12), channel_id=1, source_target_pairs={{0,2},{2,4},{4,6},{6,8},{8,10},{10,12},{12,14},{14,16},{16,18},{18... | collective-permute-start | bytes 1105928 | tf_op jit(solution)/shard_map/ppermute | solution.py:437
  37.3 28.6 %collective-permute-start.1 = (bf16[18,2,40,128]{3,2,1,0:T(8,128)(2,1)S(1)}, bf16[18,2,40,128]{3,2,1,0:T(8,128)(2,1)S(1)}, u32[]{:S(2)}, u32[]{:S(2)}) collective-permute-start(bf16[18,2,40,128]{3,2,1,0:T(8,128)(2,1)S(1)} %get-tuple-element.13), channel_id=1, source_target_pairs={{2,0},{4,2},{6,4},{8,6},{10,8},{12,10},{14,12},{16,14},{18,16},{20... | collective-permute-start | bytes 1105928 | tf_op jit(solution)/shard_map/ppermute | solution.py:438
  47.2 29.1 %collective-permute-start.4 = (bf16[18,2,40,128]{3,2,1,0:T(8,128)(2,1)S(1)}, bf16[18,2,40,128]{3,2,1,0:T(8,128)(2,1)S(1)}, u32[]{:S(2)}, u32[]{:S(2)}) collective-permute-start(bf16[18,2,40,128]{3,2,1,0:T(8,128)(2,1)S(1)} %get-tuple-element.15), channel_id=1, source_target_pairs={{0,2},{2,4},{4,6},{6,8},{8,10},{10,12},{12,14},{14,16},{16,18},{18... | collective-permute-start | bytes 1105928 | tf_op jit(solution)/shard_map/ppermute | solution.py:437
  47.2 29.0 %collective-permute-start.5 = (bf16[18,2,40,128]{3,2,1,0:T(8,128)(2,1)S(1)}, bf16[18,2,40,128]{3,2,1,0:T(8,128)(2,1)S(1)}, u32[]{:S(2)}, u32[]{:S(2)}) collective-permute-start(bf16[18,2,40,128]{3,2,1,0:T(8,128)(2,1)S(1)} %get-tuple-element.16), channel_id=1, source_target_pairs={{2,0},{4,2},{6,4},{8,6},{10,8},{12,10},{14,12},{16,14},{18,16},{20... | collective-permute-start | bytes 1105928 | tf_op jit(solution)/shard_map/ppermute | solution.py:438
  54.2 8.7 %collective-permute-start.2 = (bf16[36,2,128]{2,1,0:T(2,128)(2,1)S(1)}, bf16[36,2,128]{2,1,0:T(2,128)(2,1)S(1)}, u32[]{:S(2)}, u32[]{:S(2)}) collective-permute-start(bf16[36,2,128]{2,1,0:T(2,128)(2,1)S(1)} %pad_maximum_fusion.1), channel_id=1, source_target_pairs={{0,2},{2,4},{4,6},{6,8},{8,10},{10,12},{12,14},{14,16},{16,18},{18... | collective-permute-start | bytes 55304 | tf_op jit(solution)/shard_map/ppermute | solution.py:427
  62.9 3.0 %collective-permute-start.3 = (bf16[36,2,128]{2,1,0:T(2,128)(2,1)S(1)}, bf16[36,2,128]{2,1,0:T(2,128)(2,1)S(1)}, u32[]{:S(2)}, u32[]{:S(2)}) collective-permute-start(bf16[36,2,128]{2,1,0:T(2,128)(2,1)S(1)} %pad_maximum_fusion.2), channel_id=1, source_target_pairs={{2,0},{4,2},{6,4},{8,6},{10,8},{12,10},{14,12},{16,14},{18,16},{20... | collective-permute-start | bytes 55304 | tf_op jit(solution)/shard_map/ppermute | solution.py:428
  70.8 10.4 %copy-start.7 = (s32[1024,1]{0,1:T(1,128)S(1)}, s32[1024,1]{0,1:T(1,128)}, u32[]{:S(2)}) copy-start(s32[1024,1]{0,1:T(1,128)} %param.11) | copy-start | bytes 12292
  70.8 11.0 %collective-permute-start.6 = (bf16[18,3,128,128]{3,2,1,0:T(8,128)(2,1)S(1)}, bf16[18,3,128,128]{3,2,1,0:T(8,128)(2,1)}, u32[]{:S(2)}, u32[]{:S(2)}) collective-permute-start(bf16[18,3,128,128]{3,2,1,0:T(8,128)(2,1)S(1)} %transport_second.2.refs_0_), channel_id=1, source_target_pairs={{0,1},{1,0},{2,3},{3,2},{4,5},{5,4},{6,7},{7,6},{8,9},{9,8},{10,11... | collective-permute-start | bytes 5308424 | tf_op jit(solution)/shard_map/ppermute | solution.py:443
  81.1 3.9 %collective-permute-start.7 = (bf16[18,3,128,128]{3,2,1,0:T(8,128)(2,1)S(1)}, bf16[18,3,128,128]{3,2,1,0:T(8,128)(2,1)}, u32[]{:S(2)}, u32[]{:S(2)}) collective-permute-start(bf16[18,3,128,128]{3,2,1,0:T(8,128)(2,1)S(1)} %transport_second.3.refs_1_), channel_id=1, source_target_pairs={{0,1},{1,0},{2,3},{3,2},{4,5},{5,4},{6,7},{7,6},{8,9},{9,8},{10,11... | collective-permute-start | bytes 5308424 | tf_op jit(solution)/shard_map/ppermute | solution.py:443
  95.5 3.1 %copy-start = (bf16[3,10240,128]{2,1,0:T(8,128)(2,1)}, bf16[3,10240,128]{2,1,0:T(8,128)(2,1)S(1)}, u32[]{:S(2)}) copy-start(bf16[3,10240,128]{2,1,0:T(8,128)(2,1)S(1)} %align_columns.1.value_hbm) | copy-start | bytes 23592964
Sparse Core Ops, SparseCore 0:
  29.1 73.1 all-gather.2

commit v4 on v3

--- a/solution.py
+++ b/solution.py
@@ -300,7 +300,7 @@
     per_block = lanes // levels
     tall = -(-rows // 8) * 8
 
-    @pl.loop(0, count)
+    @pl.loop(0, count, unroll=2)
     def _(k):
         block_copy(k).wait()
         for j in range(per_block):
@@ -318,7 +318,7 @@
     ).astype(F32).astype(BF16)
     for g, triple in enumerate(TRIPLES):
 
-        @pl.loop(0, width_y, unroll=16)
+        @pl.loop(0, width_y, unroll=32)
         def _(y, g=g, triple=triple):
             columns = value_ref[g, pl.ds(pl.multiple_of(y * DEPTH, DEPTH), DEPTH), :]
             columns = jnp.concatenate(

time: 134 us -> 133 us (level)
  Pallas kernels: 50.5 us -> 49 us
    pallas_call x1, Pallas kernels: 24.6 us -> 23.1 us  [solve(): pl.pallas_call(solve_kernel, in_specs=[pl.BlockSpec(memory_space=pltpu.SM...]
  transfers between devices with their start and end apart: 16 -> 16, of which waited for: 6 -> 6; matrix products, arithmetic and copies ran while one was open for 1% -> 1% of each run, Pallas kernels for 19% -> 20%
where the time goes in v4:
time: 133 us; the launch traced here: 132 us
  Pallas kernels  49 us (37%)
  starting transfers between devices  36.7 us (28%)
  waiting for transfers between devices  22.5 us (17%)
  between operations  13.6 us (10%)
  local copies, waits for them, and re-layouts  9.03 us (7%)
  other arithmetic  1.6 us (1%)
    pallas_call x1, Pallas kernels, solve(): pl.pallas_call(solve_kernel, in_specs=[pl.BlockSpec(memory_space=pltpu.SM...  23.1 us
    ppermute x7, starting transfers between devices, fetch(): return lax.ppermute(value, ELEM, pairs)  16.1 us
    ppermute x2, starting transfers between devices, body(): right = lax.ppermute(to_left, ELEM, down)  13.9 us
    pallas_call x1, Pallas kernels, align(): pl.pallas_call(functools.partial(align_kernel, len(fields)), grid=(triple...  10.4 us
    pallas_call x2, Pallas kernels, second_part(): pl.pallas_call(lambda *refs: second_kernel(step, *refs), grid=(count // s...  9.72 us
    ppermute x1, waiting for transfers between devices, body(): lax.ppermute(jnp.stack([wind_x[:, -1], wind_y[:, -1]], 1), ELEM, up)  8.53 us
    unnamed x16, local copies, waits for them, and re-layouts  7.5 us
    pallas_call x2, Pallas kernels, first_part(): pl.pallas_call(lambda *refs: first_kernel(step, *refs), grid=(count // st...  5.74 us
  transfers between devices with their start and end apart: 16, of which 6 were waited for; matrix products, arithmetic and copies ran while one was open for 1% of the time, Pallas kernels for 20%

profile of v4, /device:TPU:1, one launch (start us, length us, event | category | flops | bytes accessed | tf_op | source)
XLA Modules:
  0.0 132.3 jit_solution(14833642117666141339)
XLA Ops:
  6.5 1.1 constant_dynamic-slice_fusion.1
  7.9 6.5 %collective-permute-start.8 = (bf16[36,576]{1,0:T(8,128)(2,1)S(1)}, bf16[36,576]{1,0:T(8,128)(2,1)S(1)}, u32[]{:S(2)}, u32[]{:S(2)}) collective-permute-start(bf16[36,576]{1,0:T(8,128)(2,1)S(1)} %reshape.5), channel_id=1, source_target_pairs={{2,0},{4,2},{6,4},{8,6},{10,8},{12,10},{14,12},{0,14},{18,16},{20,... | collective-permute-start | bytes 124424 | tf_op jit(solution)/shard_map/ppermute | solution.py:394
  14.4 1.2 collective-permute-start.9
  15.5 0.4 collective-permute-start.11
  15.9 4.6 %collective-permute-start.10 = (bf16[36,576]{1,0:T(8,128)(2,1)S(1)}, bf16[36,576]{1,0:T(8,128)(2,1)S(1)}, u32[]{:S(2)}, u32[]{:S(2)}) collective-permute-start(bf16[36,576]{1,0:T(8,128)(2,1)S(1)} %reshape.5), channel_id=1, source_target_pairs={{6,0},{8,2},{10,4},{12,6},{14,8},{0,10},{2,12},{4,14},{22,16},{24,... | collective-permute-start | bytes 124424 | tf_op jit(solution)/shard_map/ppermute | solution.py:394
  20.5 2.2 %collective-permute-start.13 = (bf16[36,576]{1,0:T(8,128)(2,1)S(1)}, bf16[36,576]{1,0:T(8,128)(2,1)S(1)}, u32[]{:S(2)}, u32[]{:S(2)}) collective-permute-start(bf16[36,576]{1,0:T(8,128)(2,1)S(1)} %reshape.5), channel_id=1, source_target_pairs={{12,0},{14,2},{0,4},{2,6},{4,8},{6,10},{8,12},{10,14},{28,16},{30,... | collective-permute-start | bytes 124424 | tf_op jit(solution)/shard_map/ppermute | solution.py:394
  22.6 1.4 %collective-permute-start.14 = (bf16[36,576]{1,0:T(8,128)(2,1)S(1)}, bf16[36,576]{1,0:T(8,128)(2,1)S(1)}, u32[]{:S(2)}, u32[]{:S(2)}) collective-permute-start(bf16[36,576]{1,0:T(8,128)(2,1)S(1)} %reshape.5), channel_id=1, source_target_pairs={{14,0},{0,2},{2,4},{4,6},{6,8},{8,10},{10,12},{12,14},{30,16},{16,... | collective-permute-start | bytes 124424 | tf_op jit(solution)/shard_map/ppermute | solution.py:394
  24.0 0.1 concatenate.13
  24.2 2.3 %collective-permute-done.12 = bf16[36,576]{1,0:T(8,128)(2,1)S(1)} collective-permute-done((bf16[36,576]{1,0:T(8,128)(2,1)S(1)}, bf16[36,576]{1,0:T(8,128)(2,1)S(1)}, u32[]{:S(2)}, u32[]{:S(2)}) %collective-permute-start.12) | collective-permute-done | bytes 41504 | tf_op jit(solution)/shard_map/ppermute | solution.py:394
  26.4 1.6 %collective-permute-done.13 = bf16[36,576]{1,0:T(8,128)(2,1)S(1)} collective-permute-done((bf16[36,576]{1,0:T(8,128)(2,1)S(1)}, bf16[36,576]{1,0:T(8,128)(2,1)S(1)}, u32[]{:S(2)}, u32[]{:S(2)}) %collective-permute-start.13) | collective-permute-done | bytes 41504 | tf_op jit(solution)/shard_map/ppermute | solution.py:394
  28.1 0.1 concatenate.14
  28.2 0.8 pad_maximum_fusion
  29.0 1.8 %copy-done.1 = bf16[40,36,8,128]{3,2,1,0:T(8,128)(2,1)S(1)} copy-done((bf16[40,36,8,128]{3,2,1,0:T(8,128)(2,1)S(1)}, bf16[40,36,8,128]{3,2,1,0:T(8,128)(2,1)}, u32[]{:S(2)}) %copy-start.1) | copy-done | bytes 2949144
  30.8 0.9 copy-done.2
  31.7 0.9 copy-done.3
  32.6 0.8 copy-done.6
  33.5 2.9 %transport_first.2 = (f32[18,8,40,128]{3,2,1,0:T(8,128)S(1)}, bf16[18,2,40,128]{3,2,1,0:T(8,128)(2,1)S(1)}, bf16[18,2,40,128]{3,2,1,0:T(8,128)(2,1)S(1)}) custom-call(bf16[40,36,8,128]{3,2,1,0:T(8,128)(2,1)S(1)} %copy-done.1, bf16[36,8,128]{2,1,0:T(8,128)(2,1)S(1)} %copy-done.2, bf16[36,8,128]{2,1,0:T(8,128)(2,1)S(1)} %copy-done.3, ...), custom_call_target="tpu_custom_call" | custom-call | flops 29491200 | bytes 5898240 | tf_op jit(solution)/shard_map/transport_first/pallas_call | solution.py:175
  36.3 1.0 collective-permute-start
  37.3 7.0 %collective-permute-start.1 = (bf16[18,2,40,128]{3,2,1,0:T(8,128)(2,1)S(1)}, bf16[18,2,40,128]{3,2,1,0:T(8,128)(2,1)S(1)}, u32[]{:S(2)}, u32[]{:S(2)}) collective-permute-start(bf16[18,2,40,128]{3,2,1,0:T(8,128)(2,1)S(1)} %get-tuple-element.13), channel_id=1, source_target_pairs={{2,0},{4,2},{6,4},{8,6},{10,8},{12,10},{14,12},{16,14},{18,16},{20... | collective-permute-start | bytes 1105928 | tf_op jit(solution)/shard_map/ppermute | solution.py:438
  44.3 2.9 %transport_first.3 = (f32[18,8,40,128]{3,2,1,0:T(8,128)S(1)}, bf16[18,2,40,128]{3,2,1,0:T(8,128)(2,1)S(1)}, bf16[18,2,40,128]{3,2,1,0:T(8,128)(2,1)S(1)}) custom-call(bf16[40,36,8,128]{3,2,1,0:T(8,128)(2,1)S(1)} %copy-done.1, bf16[36,8,128]{2,1,0:T(8,128)(2,1)S(1)} %copy-done.2, bf16[36,8,128]{2,1,0:T(8,128)(2,1)S(1)} %copy-done.3, ...), custom_call_target="tpu_custom_call" | custom-call | flops 29491200 | bytes 5898240 | tf_op jit(solution)/shard_map/transport_first/pallas_call | solution.py:175
  47.2 6.9 %collective-permute-start.5 = (bf16[18,2,40,128]{3,2,1,0:T(8,128)(2,1)S(1)}, bf16[18,2,40,128]{3,2,1,0:T(8,128)(2,1)S(1)}, u32[]{:S(2)}, u32[]{:S(2)}) collective-permute-start(bf16[18,2,40,128]{3,2,1,0:T(8,128)(2,1)S(1)} %get-tuple-element.16), channel_id=1, source_target_pairs={{2,0},{4,2},{6,4},{8,6},{10,8},{12,10},{14,12},{16,14},{18,16},{20... | collective-permute-start | bytes 1105928 | tf_op jit(solution)/shard_map/ppermute | solution.py:438
  54.4 8.5 %collective-permute-done.2.refs_5_ = bf16[36,2,128]{2,1,0:T(2,128)(2,1)S(1)} collective-permute-done((bf16[36,2,128]{2,1,0:T(2,128)(2,1)S(1)}, bf16[36,2,128]{2,1,0:T(2,128)(2,1)S(1)}, u32[]{:S(2)}, u32[]{:S(2)}) %collective-permute-start.2) | collective-permute-done | bytes 18464 | tf_op jit(solution)/shard_map/ppermute | solution.py:427
  62.9 3.0 %collective-permute-done.3.refs_6_ = bf16[36,2,128]{2,1,0:T(2,128)(2,1)S(1)} collective-permute-done((bf16[36,2,128]{2,1,0:T(2,128)(2,1)S(1)}, bf16[36,2,128]{2,1,0:T(2,128)(2,1)S(1)}, u32[]{:S(2)}, u32[]{:S(2)}) %collective-permute-start.3) | collective-permute-done | bytes 18464 | tf_op jit(solution)/shard_map/ppermute | solution.py:428
  65.9 4.9 %transport_second.2.refs_0_ = bf16[18,3,128,128]{3,2,1,0:T(8,128)(2,1)S(1)} custom-call(f32[18,8,40,128]{3,2,1,0:T(8,128)S(1)} %get-tuple-element.11.refs_0_, bf16[18,2,40,128]{3,2,1,0:T(8,128)(2,1)S(1)} %collective-permute-done.refs_1_, bf16[18,2,40,128]{3,2,1,0:T(8,128)(2,1)S(1)} %collective-permute-done.1.refs_2_, bf16[36,8,128]{2,1,0:T(8,128)(2,1)S(1)} %copy-done.2, ...), custom_call_target="tpu_custom_call" | custom-call | flops 29491200 | bytes 5898240 | tf_op jit(solution)/shard_map/transport_second/pallas_call | solution.py:215
  70.8 5.4 %collective-permute-start.6 = (bf16[18,3,128,128]{3,2,1,0:T(8,128)(2,1)S(1)}, bf16[18,3,128,128]{3,2,1,0:T(8,128)(2,1)}, u32[]{:S(2)}, u32[]{:S(2)}) collective-permute-start(bf16[18,3,128,128]{3,2,1,0:T(8,128)(2,1)S(1)} %transport_second.2.refs_0_), channel_id=1, source_target_pairs={{0,1},{1,0},{2,3},{3,2},{4,5},{5,4},{6,7},{7,6},{8,9},{9,8},{10,11... | collective-permute-start | bytes 5308424 | tf_op jit(solution)/shard_map/ppermute | solution.py:443
  76.3 4.8 %transport_second.3.refs_1_ = bf16[18,3,128,128]{3,2,1,0:T(8,128)(2,1)S(1)} custom-call(f32[18,8,40,128]{3,2,1,0:T(8,128)S(1)} %get-tuple-element.14.refs_0_, bf16[18,2,40,128]{3,2,1,0:T(8,128)(2,1)S(1)} %collective-permute-done.4.refs_1_, bf16[18,2,40,128]{3,2,1,0:T(8,128)(2,1)S(1)} %collective-permute-done.5.refs_2_, bf16[36,8,128]{2,1,0:T(8,128)(2,1)S(1)} %copy-done.2, ...), custom_call_target="tpu_custom_call" | custom-call | flops 29491200 | bytes 5898240 | tf_op jit(solution)/shard_map/transport_second/pallas_call | solution.py:215
  81.2 0.6 fusion.3.pos_ref
  81.9 3.2 %collective-permute-done.7.refs_3_ = bf16[18,3,128,128]{3,2,1,0:T(8,128)(2,1)} collective-permute-done((bf16[18,3,128,128]{3,2,1,0:T(8,128)(2,1)S(1)}, bf16[18,3,128,128]{3,2,1,0:T(8,128)(2,1)}, u32[]{:S(2)}, u32[]{:S(2)}) %collective-permute-start.7) | collective-permute-done | bytes 1769504 | tf_op jit(solution)/shard_map/ppermute | solution.py:443
  85.0 10.4 %align_columns.1.value_hbm = bf16[3,10240,128]{2,1,0:T(8,128)(2,1)S(1)} custom-call(bf16[18,3,128,128]{3,2,1,0:T(8,128)(2,1)S(1)} %transport_second.2.refs_0_, bf16[18,3,128,128]{3,2,1,0:T(8,128)(2,1)S(1)} %transport_second.3.refs_1_, bf16[18,3,128,128]{3,2,1,0:T(8,128)(2,1)} %collective-permute-done.6.refs_2_, ...), custom_call_target="tpu_custom_call" | custom-call | flops 1000 | bytes 1000 | tf_op jit(solution)/shard_map/align_columns/pallas_call | solution.py:256
  95.5 3.0 %copy-done = bf16[3,10240,128]{2,1,0:T(8,128)(2,1)} copy-done((bf16[3,10240,128]{2,1,0:T(8,128)(2,1)}, bf16[3,10240,128]{2,1,0:T(8,128)(2,1)S(1)}, u32[]{:S(2)}) %copy-start) | copy-done | bytes 7864344
  98.5 3.8 %all-gather.3.cloned.1.call-done = bf16[1152,2304]{1,0:T(8,128)(2,1)} async-done(((bf16[72,2304]{1,0:T(8,128)(2,1)}), bf16[1152,2304]{1,0:T(8,128)(2,1)}) %all-gather.3.cloned.1.call-update) | async-done | bytes 5308432 | tf_op jit(solution)/shard_map/all_gather | solution.py:401
  102.4 23.1 %solve_columns.1 = bf16[40,36,8,128]{3,2,1,0:T(8,128)(2,1)} custom-call(s32[8,128]{1,0:T(8,128)} %fusion.3.pos_ref, bf16[3,10240,128]{2,1,0:T(8,128)(2,1)} %copy-done, bf16[16,72,2304]{2,1,0:T(8,128)(2,1)} %bitcast.4), custom_call_target="tpu_custom_call" | custom-call | flops 212336640 | bytes 12582912 | tf_op jit(solution)/shard_map/solve_columns/pallas_call | solution.py:359
  (34 shorter events, 0.8 us)
Async XLA Ops:
  6.5 95.8 %all-gather.3.cloned.1.call-start = ((), (), s32[]{:S(2)}) async-start(), calls=%async_computation | async-start | bytes 5640192 | tf_op jit(solution)/shard_map/all_gather | solution.py:401
  7.9 12.6 %collective-permute-start.8 = (bf16[36,576]{1,0:T(8,128)(2,1)S(1)}, bf16[36,576]{1,0:T(8,128)(2,1)S(1)}, u32[]{:S(2)}, u32[]{:S(2)}) collective-permute-start(bf16[36,576]{1,0:T(8,128)(2,1)S(1)} %reshape.5), channel_id=1, source_target_pairs={{2,0},{4,2},{6,4},{8,6},{10,8},{12,10},{14,12},{0,14},{18,16},{20,... | collective-permute-start | bytes 124424 | tf_op jit(solution)/shard_map/ppermute | solution.py:394
  14.4 8.3 %collective-permute-start.9 = (bf16[36,576]{1,0:T(8,128)(2,1)S(1)}, bf16[36,576]{1,0:T(8,128)(2,1)S(1)}, u32[]{:S(2)}, u32[]{:S(2)}) collective-permute-start(bf16[36,576]{1,0:T(8,128)(2,1)S(1)} %reshape.5), channel_id=1, source_target_pairs={{4,0},{6,2},{8,4},{10,6},{12,8},{14,10},{0,12},{2,14},{20,16},{22,... | collective-permute-start | bytes 124424 | tf_op jit(solution)/shard_map/ppermute | solution.py:394
  15.5 8.6 %collective-permute-start.11 = (bf16[36,576]{1,0:T(8,128)(2,1)S(1)}, bf16[36,576]{1,0:T(8,128)(2,1)S(1)}, u32[]{:S(2)}, u32[]{:S(2)}) collective-permute-start(bf16[36,576]{1,0:T(8,128)(2,1)S(1)} %reshape.5), channel_id=1, source_target_pairs={{8,0},{10,2},{12,4},{14,6},{0,8},{2,10},{4,12},{6,14},{24,16},{26,... | collective-permute-start | bytes 124424 | tf_op jit(solution)/shard_map/ppermute | solution.py:394
  15.9 8.1 %collective-permute-start.10 = (bf16[36,576]{1,0:T(8,128)(2,1)S(1)}, bf16[36,576]{1,0:T(8,128)(2,1)S(1)}, u32[]{:S(2)}, u32[]{:S(2)}) collective-permute-start(bf16[36,576]{1,0:T(8,128)(2,1)S(1)} %reshape.5), channel_id=1, source_target_pairs={{6,0},{8,2},{10,4},{12,6},{14,8},{0,10},{2,12},{4,14},{22,16},{24,... | collective-permute-start | bytes 124424 | tf_op jit(solution)/shard_map/ppermute | solution.py:394
  20.5 6.0 %collective-permute-start.12 = (bf16[36,576]{1,0:T(8,128)(2,1)S(1)}, bf16[36,576]{1,0:T(8,128)(2,1)S(1)}, u32[]{:S(2)}, u32[]{:S(2)}) collective-permute-start(bf16[36,576]{1,0:T(8,128)(2,1)S(1)} %reshape.5), channel_id=1, source_target_pairs={{10,0},{12,2},{14,4},{0,6},{2,8},{4,10},{6,12},{8,14},{26,16},{28,... | collective-permute-start | bytes 124424 | tf_op jit(solution)/shard_map/ppermute | solution.py:394
  20.5 7.6 %collective-permute-start.13 = (bf16[36,576]{1,0:T(8,128)(2,1)S(1)}, bf16[36,576]{1,0:T(8,128)(2,1)S(1)}, u32[]{:S(2)}, u32[]{:S(2)}) collective-permute-start(bf16[36,576]{1,0:T(8,128)(2,1)S(1)} %reshape.5), channel_id=1, source_target_pairs={{12,0},{14,2},{0,4},{2,6},{4,8},{6,10},{8,12},{10,14},{28,16},{30,... | collective-permute-start | bytes 124424 | tf_op jit(solution)/shard_map/ppermute | solution.py:394
  22.6 5.4 %collective-permute-start.14 = (bf16[36,576]{1,0:T(8,128)(2,1)S(1)}, bf16[36,576]{1,0:T(8,128)(2,1)S(1)}, u32[]{:S(2)}, u32[]{:S(2)}) collective-permute-start(bf16[36,576]{1,0:T(8,128)(2,1)S(1)} %reshape.5), channel_id=1, source_target_pairs={{14,0},{0,2},{2,4},{4,6},{6,8},{8,10},{10,12},{12,14},{30,16},{16,... | collective-permute-start | bytes 124424 | tf_op jit(solution)/shard_map/ppermute | solution.py:394
  29.0 1.8 %copy-start.1 = (bf16[40,36,8,128]{3,2,1,0:T(8,128)(2,1)S(1)}, bf16[40,36,8,128]{3,2,1,0:T(8,128)(2,1)}, u32[]{:S(2)}) copy-start(bf16[40,36,8,128]{3,2,1,0:T(8,128)(2,1)} %refs_0_.3) | copy-start | bytes 8847364
  30.8 0.9 copy-start.2
  31.7 0.9 copy-start.3
  32.6 0.8 copy-start.6
  33.4 32.5 %copy-start.4 = (bf16[256,256]{1,0:T(8,128)(2,1)S(1)}, bf16[256,256]{1,0:T(8,128)(2,1)}, u32[]{:S(2)}) copy-start(bf16[256,256]{1,0:T(8,128)(2,1)} %constant.97.clone.refs_7_) | copy-start | bytes 393220
  33.5 32.5 %copy-start.5 = (bf16[128,256]{1,0:T(8,128)(2,1)S(1)}, bf16[128,256]{1,0:T(8,128)(2,1)}, u32[]{:S(2)}) copy-start(bf16[128,256]{1,0:T(8,128)(2,1)} %constant.98.clone.refs_8_) | copy-start | bytes 196612
  36.3 29.6 %collective-permute-start = (bf16[18,2,40,128]{3,2,1,0:T(8,128)(2,1)S(1)}, bf16[18,2,40,128]{3,2,1,0:T(8,128)(2,1)S(1)}, u32[]{:S(2)}, u32[]{:S(2)}) collective-permute-start(bf16[18,2,40,128]{3,2,1,0:T(8,128)(2,1)S(1)} %get-tuple-element.12), channel_id=1, source_target_pairs={{0,2},{2,4},{4,6},{6,8},{8,10},{10,12},{12,14},{14,16},{16,18},{18... | collective-permute-start | bytes 1105928 | tf_op jit(solution)/shard_map/ppermute | solution.py:437
  37.3 28.6 %collective-permute-start.1 = (bf16[18,2,40,128]{3,2,1,0:T(8,128)(2,1)S(1)}, bf16[18,2,40,128]{3,2,1,0:T(8,128)(2,1)S(1)}, u32[]{:S(2)}, u32[]{:S(2)}) collective-permute-start(bf16[18,2,40,128]{3,2,1,0:T(8,128)(2,1)S(1)} %get-tuple-element.13), channel_id=1, source_target_pairs={{2,0},{4,2},{6,4},{8,6},{10,8},{12,10},{14,12},{16,14},{18,16},{20... | collective-permute-start | bytes 1105928 | tf_op jit(solution)/shard_map/ppermute | solution.py:438
  47.2 29.1 %collective-permute-start.4 = (bf16[18,2,40,128]{3,2,1,0:T(8,128)(2,1)S(1)}, bf16[18,2,40,128]{3,2,1,0:T(8,128)(2,1)S(1)}, u32[]{:S(2)}, u32[]{:S(2)}) collective-permute-start(bf16[18,2,40,128]{3,2,1,0:T(8,128)(2,1)S(1)} %get-tuple-element.15), channel_id=1, source_target_pairs={{0,2},{2,4},{4,6},{6,8},{8,10},{10,12},{12,14},{14,16},{16,18},{18... | collective-permute-start | bytes 1105928 | tf_op jit(solution)/shard_map/ppermute | solution.py:437
  47.2 29.0 %collective-permute-start.5 = (bf16[18,2,40,128]{3,2,1,0:T(8,128)(2,1)S(1)}, bf16[18,2,40,128]{3,2,1,0:T(8,128)(2,1)S(1)}, u32[]{:S(2)}, u32[]{:S(2)}) collective-permute-start(bf16[18,2,40,128]{3,2,1,0:T(8,128)(2,1)S(1)} %get-tuple-element.16), channel_id=1, source_target_pairs={{2,0},{4,2},{6,4},{8,6},{10,8},{12,10},{14,12},{16,14},{18,16},{20... | collective-permute-start | bytes 1105928 | tf_op jit(solution)/shard_map/ppermute | solution.py:438
  54.2 8.7 %collective-permute-start.2 = (bf16[36,2,128]{2,1,0:T(2,128)(2,1)S(1)}, bf16[36,2,128]{2,1,0:T(2,128)(2,1)S(1)}, u32[]{:S(2)}, u32[]{:S(2)}) collective-permute-start(bf16[36,2,128]{2,1,0:T(2,128)(2,1)S(1)} %pad_maximum_fusion.1), channel_id=1, source_target_pairs={{0,2},{2,4},{4,6},{6,8},{8,10},{10,12},{12,14},{14,16},{16,18},{18... | collective-permute-start | bytes 55304 | tf_op jit(solution)/shard_map/ppermute | solution.py:427
  62.9 3.0 %collective-permute-start.3 = (bf16[36,2,128]{2,1,0:T(2,128)(2,1)S(1)}, bf16[36,2,128]{2,1,0:T(2,128)(2,1)S(1)}, u32[]{:S(2)}, u32[]{:S(2)}) collective-permute-start(bf16[36,2,128]{2,1,0:T(2,128)(2,1)S(1)} %pad_maximum_fusion.2), channel_id=1, source_target_pairs={{2,0},{4,2},{6,4},{8,6},{10,8},{12,10},{14,12},{16,14},{18,16},{20... | collective-permute-start | bytes 55304 | tf_op jit(solution)/shard_map/ppermute | solution.py:428
  70.8 10.4 %copy-start.7 = (s32[1024,1]{0,1:T(1,128)S(1)}, s32[1024,1]{0,1:T(1,128)}, u32[]{:S(2)}) copy-start(s32[1024,1]{0,1:T(1,128)} %param.11) | copy-start | bytes 12292
  70.8 11.0 %collective-permute-start.6 = (bf16[18,3,128,128]{3,2,1,0:T(8,128)(2,1)S(1)}, bf16[18,3,128,128]{3,2,1,0:T(8,128)(2,1)}, u32[]{:S(2)}, u32[]{:S(2)}) collective-permute-start(bf16[18,3,128,128]{3,2,1,0:T(8,128)(2,1)S(1)} %transport_second.2.refs_0_), channel_id=1, source_target_pairs={{0,1},{1,0},{2,3},{3,2},{4,5},{5,4},{6,7},{7,6},{8,9},{9,8},{10,11... | collective-permute-start | bytes 5308424 | tf_op jit(solution)/shard_map/ppermute | solution.py:443
  81.1 3.9 %collective-permute-start.7 = (bf16[18,3,128,128]{3,2,1,0:T(8,128)(2,1)S(1)}, bf16[18,3,128,128]{3,2,1,0:T(8,128)(2,1)}, u32[]{:S(2)}, u32[]{:S(2)}) collective-permute-start(bf16[18,3,128,128]{3,2,1,0:T(8,128)(2,1)S(1)} %transport_second.3.refs_1_), channel_id=1, source_target_pairs={{0,1},{1,0},{2,3},{3,2},{4,5},{5,4},{6,7},{7,6},{8,9},{9,8},{10,11... | collective-permute-start | bytes 5308424 | tf_op jit(solution)/shard_map/ppermute | solution.py:443
  95.5 3.1 %copy-start = (bf16[3,10240,128]{2,1,0:T(8,128)(2,1)}, bf16[3,10240,128]{2,1,0:T(8,128)(2,1)S(1)}, u32[]{:S(2)}) copy-start(bf16[3,10240,128]{2,1,0:T(8,128)(2,1)S(1)} %align_columns.1.value_hbm) | copy-start | bytes 23592964
Sparse Core Ops, SparseCore 0:
  29.1 73.1 all-gather.2
